TPU v7x, 128 devices: a whole 4x4x4 slice. The times are simulated.
128 devices in a mesh: band: 16 (over z, x), patch: 8 (over y, core).
Axes of the slice: x: 4, y: 4, z: 4, core: 2. Of those that a mesh axis runs over, the one named last changes fastest.
Arguments:
- grid_latent: bfloat16 [32768, 512], P(('band', 'patch')), may hold values from -6 to 6
- mesh_latent: bfloat16 [16384, 512], P(('band', 'patch')), may hold values from -6 to 6
- grid_cotangent: bfloat16 [32768, 512], P(('band', 'patch')), may hold values from -6 to 6
- enc_w_send: bfloat16 [512, 512], replicated, may hold values from -0.25 to 0.25
- enc_w_recv: bfloat16 [512, 512], replicated, may hold values from -0.25 to 0.25
- enc_w_out: bfloat16 [512, 512], replicated, may hold values from -0.25 to 0.25
- dec_w_send: bfloat16 [512, 512], replicated, may hold values from -0.25 to 0.25
- dec_w_recv: bfloat16 [512, 512], replicated, may hold values from -0.25 to 0.25
- dec_w_out: bfloat16 [512, 512], replicated, may hold values from -0.25 to 0.25
- enc_sender: int32 [128, 3, 8, 32], P(('band', 'patch')), may hold values from 0 to 255
- enc_receiver: int32 [128, 3, 8, 32], P(('band', 'patch')), may hold values from 0 to 127
- enc_count: int32 [128, 3, 8], P(('band', 'patch')), may hold values from 0 to 32, as said below
- dec_sender: int32 [128, 3, 8, 32], P(('band', 'patch')), may hold values from 0 to 127
- dec_receiver: int32 [128, 3, 8, 32], P(('band', 'patch')), may hold values from 0 to 255
- dec_count: int32 [128, 3, 8], P(('band', 'patch')), may hold values from 0 to 32, as said below
Outputs:
- grid_grad: float32 [32768, 512], P(('band', 'patch'))
- mesh_grad: float32 [16384, 512], P(('band', 'patch'))
- grad_enc_send: float32 [512, 512], replicated
- grad_enc_recv: float32 [512, 512], replicated
- grad_enc_out: float32 [512, 512], replicated
- grad_dec_send: float32 [512, 512], replicated
- grad_dec_recv: float32 [512, 512], replicated
- grad_dec_out: float32 [512, 512], replicated
Inputs may be any that keep to these rules, and one draw needn't show every extreme that they name: enc_count[m, o, p] is 0 exactly where the source band b - o + 1 lies outside the bands, and at least 1 elsewhere; one mesh device holds 32 live slots from every source device that it has. dec_count[d, o, q] is 0 exactly where the source band b - o + 1 lies outside the bands, and at least 1 elsewhere; one grid device holds 32 live slots from every source device that it has.
All inputs are finite; a program needn't handle non-finite values.
Results may differ from a plain program's by a relative error of at most 0.0095.
Values may be sent and summed in bfloat16 or wider, within the bound.
A program may use at most 64 MiB of HBM per device.

v0:
```python
import jax
import jax.numpy as jnp
from jax import lax
from jax.sharding import PartitionSpec as P


def from_behind(block, axis, distance):
    devices = range(lax.axis_size(axis))
    route = [(i - distance, i) for i in devices if i - distance in devices]
    return lax.ppermute(block, axis, route)


def product(left, right):
    return jnp.dot(left, right, preferred_element_type=jnp.float32)


def product_back(left, weight):
    return lax.dot_general(
        left, weight, (((1,), (1,)), ((), ())), preferred_element_type=jnp.float32
    )


def outer_sum(left, right):
    return lax.dot_general(
        left, right, (((0,), (0,)), ((), ())), preferred_element_type=jnp.float32
    )


def silu_slope(value):
    sigma = jax.nn.sigmoid(value)
    return sigma * (1.0 + value * (1.0 - sigma))


def patch_move(rows):
    return lax.all_to_all(rows, "patch", split_axis=1, concat_axis=1, tiled=True)


def band_forward(rows):
    pieces = []
    for offset in range(3):
        if offset == 1:
            pieces.append(rows[1])
        else:
            pieces.append(from_behind(rows[offset], "band", offset - 1))
    return jnp.stack(pieces)


def band_backward(rows):
    return band_forward(rows[::-1])[::-1]


def send_out(rows):
    return band_forward(patch_move(rows))


def send_back(rows):
    return patch_move(band_backward(rows))


def per_device(
    grid_latent,
    mesh_latent,
    grid_cotangent,
    enc_w_send,
    enc_w_recv,
    enc_w_out,
    dec_w_send,
    dec_w_recv,
    dec_w_out,
    enc_sender,
    enc_receiver,
    enc_count,
    dec_sender,
    dec_receiver,
    dec_count,
):
    bands = lax.axis_size("band")
    patches = lax.axis_size("patch")
    devices = bands * patches
    width = grid_latent.shape[1]
    grid_nodes = grid_latent.shape[0]
    mesh_nodes = mesh_latent.shape[0]
    slots = enc_sender.shape[3]
    flat = 3 * patches * slots
    slot_ids = jnp.arange(slots, dtype=jnp.int32)
    enc_live = (slot_ids[None, None, :] < enc_count[0][:, :, None]).reshape(flat, 1)
    dec_live = (slot_ids[None, None, :] < dec_count[0][:, :, None]).reshape(flat, 1)
    enc_source = enc_sender[0].reshape(flat)
    enc_target = enc_receiver[0].reshape(flat)
    dec_source = dec_sender[0].reshape(flat)
    dec_target = dec_receiver[0].reshape(flat)
    sender_rows = send_out(grid_latent[enc_sender[0]]).reshape(flat, width)
    receiver_rows = mesh_latent[enc_target]
    enc_pre = product(sender_rows, enc_w_send) + product(receiver_rows, enc_w_recv)
    enc_act = jax.nn.silu(enc_pre).astype(jnp.bfloat16)
    enc_msg = jnp.where(enc_live, product(enc_act, enc_w_out), jnp.float32(0.0))
    mesh_new = (
        mesh_latent.astype(jnp.float32) + jax.ops.segment_sum(enc_msg, enc_target, mesh_nodes)
    ).astype(jnp.bfloat16)
    mesh_rows = send_out(mesh_new[dec_sender[0]]).reshape(flat, width)
    grid_rows = grid_latent[dec_target]
    dec_pre = product(mesh_rows, dec_w_send) + product(grid_rows, dec_w_recv)
    dec_act = jax.nn.silu(dec_pre).astype(jnp.bfloat16)
    dec_gmsg = jnp.where(dec_live, grid_cotangent[dec_target], jnp.zeros((), jnp.bfloat16))
    dec_dpre = (product_back(dec_gmsg, dec_w_out) * silu_slope(dec_pre)).astype(jnp.bfloat16)
    dec_dsend = (
        product_back(dec_dpre, dec_w_send).astype(jnp.bfloat16).reshape(3, patches, slots, width)
    )
    mesh_return = send_back(dec_dsend).reshape(flat, width)
    grid_from_decoder = jax.ops.segment_sum(
        product_back(dec_dpre, dec_w_recv), dec_target, grid_nodes
    )
    grad_dec_send = outer_sum(mesh_rows, dec_dpre)
    grad_dec_recv = outer_sum(grid_rows, dec_dpre)
    grad_dec_out = outer_sum(dec_act, dec_gmsg)
    mesh_grad_new = jax.ops.segment_sum(mesh_return.astype(jnp.float32), dec_source, mesh_nodes)
    enc_gmsg = jnp.where(
        enc_live, mesh_grad_new.astype(jnp.bfloat16)[enc_target], jnp.zeros((), jnp.bfloat16)
    )
    enc_dpre = (product_back(enc_gmsg, enc_w_out) * silu_slope(enc_pre)).astype(jnp.bfloat16)
    enc_dsend = (
        product_back(enc_dpre, enc_w_send).astype(jnp.bfloat16).reshape(3, patches, slots, width)
    )
    grid_return = send_back(enc_dsend).reshape(flat, width)
    mesh_grad = mesh_grad_new + jax.ops.segment_sum(
        product_back(enc_dpre, enc_w_recv), enc_target, mesh_nodes
    )
    grad_enc_send = outer_sum(sender_rows, enc_dpre)
    grad_enc_recv = outer_sum(receiver_rows, enc_dpre)
    grad_enc_out = outer_sum(enc_act, enc_gmsg)
    grid_grad = grid_cotangent.astype(jnp.float32) + grid_from_decoder
    grid_grad = grid_grad + jax.ops.segment_sum(
        grid_return.astype(jnp.float32), enc_source, grid_nodes
    )
    factor = float(devices * 3 * patches * slots) ** (-0.5)
    totals = lax.psum(
        (
            grad_enc_send * factor,
            grad_enc_recv * factor,
            grad_enc_out * factor,
            grad_dec_send * factor,
            grad_dec_recv * factor,
            grad_dec_out * factor,
        ),
        ("band", "patch"),
    )
    return (grid_grad, mesh_grad, totals[0], totals[1], totals[2], totals[3], totals[4], totals[5])


def solution(mesh):
    in_specs = (
        P(("band", "patch"), None),
        P(("band", "patch"), None),
        P(("band", "patch"), None),
        P(),
        P(),
        P(),
        P(),
        P(),
        P(),
        P(("band", "patch"), None, None, None),
        P(("band", "patch"), None, None, None),
        P(("band", "patch"), None, None),
        P(("band", "patch"), None, None, None),
        P(("band", "patch"), None, None, None),
        P(("band", "patch"), None, None),
    )
    out_specs = (
        P(("band", "patch"), None),
        P(("band", "patch"), None),
        P(),
        P(),
        P(),
        P(),
        P(),
        P(),
    )
    return jax.shard_map(
        per_device, mesh=mesh, in_specs=in_specs, out_specs=out_specs, check_vma=False
    )
```

profile of v0, /device:TPU:1, one launch (start us, length us, event | category | flops | bytes accessed | tf_op | source)
XLA Modules:
  0.0 332.3 jit_solution(11984119101719216064)
XLA Ops:
  8.0 3.7 %gather_fusion.1 = bf16[768,512]{1,0:T(8,128)(2,1)S(1)} fusion(bf16[256,512]{1,0:T(8,128)(2,1)} %param.15, s32[1024]{0:T(1024)S(1)} %pad_clamp_fusion.2), kind=kCustom, calls=%fused_computation.1 | custom fusion | bytes 1575936 | tf_op jit(solution)/shard_map/gather | solution.py:92
  12.7 6.0 %all-to-all-start = ((bf16[3,8,32,512]{3,2,0,1:T(8,128)(2,1)}), bf16[3,8,32,512]{3,2,0,1:T(8,128)(2,1)S(1)}, u32[]{:S(2)}, u32[]{:S(2)}) async-start(bf16[3,8,32,512]{3,2,0,1:T(8,128)(2,1)} %copy.32), calls=%async_computation | async-start | bytes 1572864 | tf_op jit(solution)/shard_map/all_to_all | solution.py:35
  21.9 9.1 %all-to-all-done = bf16[3,8,32,512]{3,2,0,1:T(8,128)(2,1)S(1)} async-done(((bf16[3,8,32,512]{3,2,0,1:T(8,128)(2,1)}), bf16[3,8,32,512]{3,2,0,1:T(8,128)(2,1)S(1)}, u32[]{:S(2)}, u32[]{:S(2)}) %all-to-all-start) | async-done | bytes 786464 | tf_op jit(solution)/shard_map/all_to_all | solution.py:35
  38.9 4.0 %collective-permute-done = bf16[8,32,512]{2,1,0:T(8,128)(2,1)S(1)} collective-permute-done((bf16[8,32,512]{2,1,0:T(8,128)(2,1)S(1)}, bf16[8,32,512]{2,1,0:T(8,128)(2,1)S(1)}, u32[]{:S(2)}, u32[]{:S(2)}) %collective-permute-start) | collective-permute-done | bytes 262176 | tf_op jit(solution)/shard_map/ppermute | solution.py:10
  44.7 3.1 fusion.16
  47.9 9.2 %scatter_custom_fusion = f32[128,512]{1,0:T(8,128)S(1)} fusion(f32[128,512]{1,0:T(8,128)S(1)} %convert_element_type.43, s32[768]{0:T(1024)S(1)} %reshape.238, f32[768,512]{1,0:T(8,128)} %fusion.16, f32[]{:T(128)} %constant.12.clone.1, pred[768]{0:T(1024)(128)(4,1)S(1)} %lt.96), kind=kCustom, calls=%fused_computation.17 | custom fusion | flops 786432 | bytes 1836036 | tf_op jit(solution)/shard_map/scatter-add | solution.py:98
  60.8 6.2 %all-to-all-start.1 = ((bf16[3,8,32,512]{3,2,0,1:T(8,128)(2,1)}), bf16[3,8,32,512]{3,2,0,1:T(8,128)(2,1)}, u32[]{:S(2)}, u32[]{:S(2)}) async-start(bf16[3,8,32,512]{3,2,0,1:T(8,128)(2,1)} %copy.35), calls=%async_computation.1 | async-start | bytes 1572864 | tf_op jit(solution)/shard_map/all_to_all | solution.py:35
  69.9 3.3 gather_fusion
  73.4 6.0 %all-to-all-done.1 = bf16[3,8,32,512]{3,2,0,1:T(8,128)(2,1)} async-done(((bf16[3,8,32,512]{3,2,0,1:T(8,128)(2,1)}), bf16[3,8,32,512]{3,2,0,1:T(8,128)(2,1)}, u32[]{:S(2)}, u32[]{:S(2)}) %all-to-all-start.1) | async-done | bytes 786464 | tf_op jit(solution)/shard_map/all_to_all | solution.py:35
  88.4 3.8 %collective-permute-done.2 = bf16[8,32,512]{2,1,0:T(8,128)(2,1)S(1)} collective-permute-done((bf16[8,32,512]{2,1,0:T(8,128)(2,1)S(1)}, bf16[8,32,512]{2,1,0:T(8,128)(2,1)S(1)}, u32[]{:S(2)}, u32[]{:S(2)}) %collective-permute-start.2) | collective-permute-done | bytes 262176 | tf_op jit(solution)/shard_map/ppermute | solution.py:10
  95.4 5.3 %collective-permute-start.5 = (bf16[8,32,512]{2,1,0:T(8,128)(2,1)S(1)}, bf16[8,32,512]{2,1,0:T(8,128)(2,1)S(1)}, u32[]{:S(2)}, u32[]{:S(2)}) collective-permute-start(bf16[8,32,512]{2,1,0:T(8,128)(2,1)S(1)} %bitcast.114), channel_id=1, source_target_pairs={{0,8},{8,16},{16,24},{24,32},{32,40},{40,48},{48,56},{56,64},{64,7... | collective-permute-start | bytes 786440 | tf_op jit(solution)/shard_map/ppermute | solution.py:10
  104.5 3.8 %collective-permute-done.4 = bf16[8,32,512]{2,1,0:T(8,128)(2,1)S(1)} collective-permute-done((bf16[8,32,512]{2,1,0:T(8,128)(2,1)S(1)}, bf16[8,32,512]{2,1,0:T(8,128)(2,1)S(1)}, u32[]{:S(2)}, u32[]{:S(2)}) %collective-permute-start.4) | collective-permute-done | bytes 262176 | tf_op jit(solution)/shard_map/ppermute | solution.py:10
  109.4 6.4 %all-to-all-start.2 = ((bf16[3,8,32,512]{3,2,0,1:T(8,128)(2,1)}), bf16[3,8,32,512]{3,2,0,1:T(8,128)(2,1)S(1)}, u32[]{:S(2)}, u32[]{:S(2)}) async-start(bf16[3,8,32,512]{3,2,0,1:T(8,128)(2,1)} %rev.8), calls=%async_computation.2 | async-start | bytes 1572864 | tf_op jit(solution)/shard_map/all_to_all | solution.py:35
  120.5 7.7 %all-to-all-done.2 = bf16[3,8,32,512]{3,2,0,1:T(8,128)(2,1)S(1)} async-done(((bf16[3,8,32,512]{3,2,0,1:T(8,128)(2,1)}), bf16[3,8,32,512]{3,2,0,1:T(8,128)(2,1)S(1)}, u32[]{:S(2)}, u32[]{:S(2)}) %all-to-all-start.2) | async-done | bytes 786464 | tf_op jit(solution)/shard_map/all_to_all | solution.py:35
  129.5 7.3 %scatter_custom_fusion.2 = f32[128,512]{1,0:T(8,128)S(1)} fusion(s32[768]{0:T(1024)S(1)} %reshape.254, f32[768,512]{1,0:T(8,128)} %bitcast.105, f32[]{:T(128)} %constant.12.clone.1), kind=kCustom, calls=%fused_computation.46 | custom fusion | flops 393216 | bytes 262656 | tf_op jit(solution)/shard_map/scatter-add | solution.py:116
  145.3 3.1 convolution_multiply_fusion.3
  150.4 4.0 %collective-permute-start.7 = (bf16[8,32,512]{2,1,0:T(8,128)(2,1)S(1)}, bf16[8,32,512]{2,1,0:T(8,128)(2,1)S(1)}, u32[]{:S(2)}, u32[]{:S(2)}) collective-permute-start(bf16[8,32,512]{2,1,0:T(8,128)(2,1)S(1)} %bitcast.118), channel_id=1, source_target_pairs={{0,8},{8,16},{16,24},{24,32},{32,40},{40,48},{48,56},{56,64},{64,7... | collective-permute-start | bytes 786440 | tf_op jit(solution)/shard_map/ppermute | solution.py:10
  155.8 3.4 %collective-permute-done.7 = bf16[8,32,512]{2,1,0:T(8,128)(2,1)S(1)} collective-permute-done((bf16[8,32,512]{2,1,0:T(8,128)(2,1)S(1)}, bf16[8,32,512]{2,1,0:T(8,128)(2,1)S(1)}, u32[]{:S(2)}, u32[]{:S(2)}) %collective-permute-start.7) | collective-permute-done | bytes 262176 | tf_op jit(solution)/shard_map/ppermute | solution.py:10
  159.2 4.7 %collective-permute-done.6 = bf16[8,32,512]{2,1,0:T(8,128)(2,1)S(1)} collective-permute-done((bf16[8,32,512]{2,1,0:T(8,128)(2,1)S(1)}, bf16[8,32,512]{2,1,0:T(8,128)(2,1)S(1)}, u32[]{:S(2)}, u32[]{:S(2)}) %collective-permute-start.6) | collective-permute-done | bytes 262176 | tf_op jit(solution)/shard_map/ppermute | solution.py:10
  164.9 6.9 %all-to-all-start.3 = ((bf16[3,8,32,512]{3,2,0,1:T(8,128)(2,1)}), bf16[3,8,32,512]{3,2,0,1:T(8,128)(2,1)}, u32[]{:S(2)}, u32[]{:S(2)}) async-start(bf16[3,8,32,512]{3,2,0,1:T(8,128)(2,1)} %rev.9), calls=%async_computation.3 | async-start | bytes 1572864 | tf_op jit(solution)/shard_map/all_to_all | solution.py:35
  173.9 6.8 %scatter_fusion = f32[256,512]{1,0:T(8,128)S(1)} fusion(f32[256,512]{1,0:T(8,128)S(1)} %convert_element_type.42, s32[768]{0:T(1024)S(1)} %reshape.246, f32[768,512]{1,0:T(8,128)S(1)} %fusion.21), kind=kCustom, calls=%fused_computation.7 | custom fusion | flops 393216 | bytes 4721664 | tf_op jit(solution)/shard_map/scatter-add | solution.py:110
  182.5 6.7 %scatter_fusion.1 = f32[128,512]{1,0:T(8,128)S(1)} fusion(f32[128,512]{1,0:T(8,128)S(1)} %scatter_custom_fusion.2, s32[768]{0:T(1024)S(1)} %reshape.238, f32[768,512]{1,0:T(8,128)S(1)} %fusion.22), kind=kCustom, calls=%fused_computation.10 | custom fusion | flops 393216 | bytes 4721664 | tf_op jit(solution)/shard_map/scatter-add | solution.py:125
  190.5 7.0 %scatter_custom_fusion.3 = f32[256,512]{1,0:T(8,128)S(1)} fusion(s32[768]{0:T(1024)S(1)} %reshape.262, bf16[768,512]{1,0:T(8,128)(2,1)S(1)} %bitcast.98, f32[]{:T(128)} %constant.12.clone.1), kind=kCustom, calls=%fused_computation.11 | custom fusion | flops 786432 | bytes 1310724 | tf_op jit(solution)/shard_map/scatter-add | solution.py:132
  198.4 117.9 %all-reduce.3.cloned.1.call-done = (f32[512,512]{1,0:T(8,128)}, f32[512,512]{1,0:T(8,128)}, f32[512,512]{1,0:T(8,128)}, f32[512,512]{1,0:T(8,128)}, f32[512,512]{1,0:T(8,128)}, /*index=5*/f32[512,512]{1,0:T(8,128)}) async-done(((f32[512,512]{1,0:T(8,128)}, f32[512,512]{1,0:T(8,128)}, f32[512,512]{1,0:T(8,128)}, f32[512,512]{1,0:T(8,128)}, f32[512,512]{1,0:T(8,128)}, /*index=5*/f32[512,512]{1,0:T(8,128)}), ...) | async-done | bytes 6291472 | tf_op jit(solution)/shard_map/psum | solution.py:136
  (144 shorter events, 72.1 us)
Async XLA Ops:
  7.2 85.1 %copy-start = (bf16[512,512]{1,0:T(8,128)(2,1)S(1)}, bf16[512,512]{1,0:T(8,128)(2,1)}, u32[]{:S(2)}) copy-start(bf16[512,512]{1,0:T(8,128)(2,1)} %param.21) | copy-start | bytes 1572868
  11.7 7.1 %copy-start.3 = (bf16[128,512]{1,0:T(8,128)(2,1)S(1)}, bf16[128,512]{1,0:T(8,128)(2,1)}, u32[]{:S(2)}) copy-start(bf16[128,512]{1,0:T(8,128)(2,1)} %param.16) | copy-start | bytes 393220
  12.7 18.3 %all-to-all-start = ((bf16[3,8,32,512]{3,2,0,1:T(8,128)(2,1)}), bf16[3,8,32,512]{3,2,0,1:T(8,128)(2,1)S(1)}, u32[]{:S(2)}, u32[]{:S(2)}) async-start(bf16[3,8,32,512]{3,2,0,1:T(8,128)(2,1)} %copy.32), calls=%async_computation | async-start | bytes 1572864 | tf_op jit(solution)/shard_map/all_to_all | solution.py:35
  21.6 14.0 %copy-start.9 = (bf16[512,512]{1,0:T(8,128)(2,1)S(1)}, bf16[512,512]{1,0:T(8,128)(2,1)}, u32[]{:S(2)}) copy-start(bf16[512,512]{1,0:T(8,128)(2,1)} %param.19) | copy-start | bytes 1572868
  31.0 7.9 %collective-permute-start.1 = (bf16[8,32,512]{2,1,0:T(8,128)(2,1)S(1)}, bf16[8,32,512]{2,1,0:T(8,128)(2,1)S(1)}, u32[]{:S(2)}, u32[]{:S(2)}) collective-permute-start(bf16[8,32,512]{2,1,0:T(8,128)(2,1)S(1)} %get-tuple-element.24), channel_id=1, source_target_pairs={{0,8},{8,16},{16,24},{24,32},{32,40},{40,48},{48,56},{56,64},{64,7... | collective-permute-start | bytes 786440 | tf_op jit(solution)/shard_map/ppermute | solution.py:10
  34.2 8.8 %copy-start.23 = (bf16[512,512]{1,0:T(8,128)(2,1)S(1)}, bf16[512,512]{1,0:T(8,128)(2,1)}, u32[]{:S(2)}) copy-start(bf16[512,512]{1,0:T(8,128)(2,1)} %param.18) | copy-start | bytes 1572868
  34.2 8.7 %collective-permute-start = (bf16[8,32,512]{2,1,0:T(8,128)(2,1)S(1)}, bf16[8,32,512]{2,1,0:T(8,128)(2,1)S(1)}, u32[]{:S(2)}, u32[]{:S(2)}) collective-permute-start(bf16[8,32,512]{2,1,0:T(8,128)(2,1)S(1)} %get-tuple-element.23), channel_id=1, source_target_pairs={{8,0},{16,8},{24,16},{32,24},{40,32},{48,40},{56,48},{64,56},{72,6... | collective-permute-start | bytes 786440 | tf_op jit(solution)/shard_map/ppermute | solution.py:10
  59.8 7.2 %copy-start.28 = (s32[1,3,8,32]{3,2,1,0:T(8,128)S(1)}, s32[1,3,8,32]{3,2,1,0:T(8,128)}, u32[]{:S(2)}) copy-start(s32[1,3,8,32]{3,2,1,0:T(8,128)} %param.28) | copy-start | bytes 9220
  59.8 7.3 %copy-start.2 = (bf16[256,512]{1,0:T(8,128)(2,1)S(1)}, bf16[256,512]{1,0:T(8,128)(2,1)}, u32[]{:S(2)}) copy-start(bf16[256,512]{1,0:T(8,128)(2,1)} %param.15) | copy-start | bytes 786436
  60.8 18.6 %all-to-all-start.1 = ((bf16[3,8,32,512]{3,2,0,1:T(8,128)(2,1)}), bf16[3,8,32,512]{3,2,0,1:T(8,128)(2,1)}, u32[]{:S(2)}, u32[]{:S(2)}) async-start(bf16[3,8,32,512]{3,2,0,1:T(8,128)(2,1)} %copy.35), calls=%async_computation.1 | async-start | bytes 1572864 | tf_op jit(solution)/shard_map/all_to_all | solution.py:35
  73.2 12.0 %copy-start.7 = (bf16[512,512]{1,0:T(8,128)(2,1)S(1)}, bf16[512,512]{1,0:T(8,128)(2,1)}, u32[]{:S(2)}) copy-start(bf16[512,512]{1,0:T(8,128)(2,1)} %param.22) | copy-start | bytes 1572868
  80.5 7.8 %collective-permute-start.3 = (bf16[8,32,512]{2,1,0:T(8,128)(2,1)S(1)}, bf16[8,32,512]{2,1,0:T(8,128)(2,1)S(1)}, u32[]{:S(2)}, u32[]{:S(2)}) collective-permute-start(bf16[8,32,512]{2,1,0:T(8,128)(2,1)S(1)} %get-tuple-element.21), channel_id=1, source_target_pairs={{0,8},{8,16},{16,24},{24,32},{32,40},{40,48},{48,56},{56,64},{64,7... | collective-permute-start | bytes 786440 | tf_op jit(solution)/shard_map/ppermute | solution.py:10
  83.7 8.5 %collective-permute-start.2 = (bf16[8,32,512]{2,1,0:T(8,128)(2,1)S(1)}, bf16[8,32,512]{2,1,0:T(8,128)(2,1)S(1)}, u32[]{:S(2)}, u32[]{:S(2)}) collective-permute-start(bf16[8,32,512]{2,1,0:T(8,128)(2,1)S(1)} %get-tuple-element.20), channel_id=1, source_target_pairs={{8,0},{16,8},{24,16},{32,24},{40,32},{48,40},{56,48},{64,56},{72,6... | collective-permute-start | bytes 786440 | tf_op jit(solution)/shard_map/ppermute | solution.py:10
  94.7 13.7 %copy-start.20 = (bf16[768,512]{1,0:T(8,128)(2,1)}, bf16[768,512]{1,0:T(8,128)(2,1)S(1)}, u32[]{:S(2)}) copy-start(bf16[768,512]{1,0:T(8,128)(2,1)S(1)} %multiply_convert_fusion.2) | copy-start | bytes 2359300
  95.4 9.1 %collective-permute-start.5 = (bf16[8,32,512]{2,1,0:T(8,128)(2,1)S(1)}, bf16[8,32,512]{2,1,0:T(8,128)(2,1)S(1)}, u32[]{:S(2)}, u32[]{:S(2)}) collective-permute-start(bf16[8,32,512]{2,1,0:T(8,128)(2,1)S(1)} %bitcast.114), channel_id=1, source_target_pairs={{0,8},{8,16},{16,24},{24,32},{32,40},{40,48},{48,56},{56,64},{64,7... | collective-permute-start | bytes 786440 | tf_op jit(solution)/shard_map/ppermute | solution.py:10
  100.8 7.6 %collective-permute-start.4 = (bf16[8,32,512]{2,1,0:T(8,128)(2,1)S(1)}, bf16[8,32,512]{2,1,0:T(8,128)(2,1)S(1)}, u32[]{:S(2)}, u32[]{:S(2)}) collective-permute-start(bf16[8,32,512]{2,1,0:T(8,128)(2,1)S(1)} %bitcast.108), channel_id=1, source_target_pairs={{8,0},{16,8},{24,16},{32,24},{40,32},{48,40},{56,48},{64,56},{72,6... | collective-permute-start | bytes 786440 | tf_op jit(solution)/shard_map/ppermute | solution.py:10
  109.4 18.7 %all-to-all-start.2 = ((bf16[3,8,32,512]{3,2,0,1:T(8,128)(2,1)}), bf16[3,8,32,512]{3,2,0,1:T(8,128)(2,1)S(1)}, u32[]{:S(2)}, u32[]{:S(2)}) async-start(bf16[3,8,32,512]{3,2,0,1:T(8,128)(2,1)} %rev.8), calls=%async_computation.2 | async-start | bytes 1572864 | tf_op jit(solution)/shard_map/all_to_all | solution.py:35
  115.9 200.4 %all-reduce.3.cloned.1.call-start = ((), (), s32[]{:S(2)}) async-start(), calls=%async_computation.4 | async-start | bytes 12582912 | tf_op jit(solution)/shard_map/psum | solution.py:136
  150.4 8.8 %collective-permute-start.7 = (bf16[8,32,512]{2,1,0:T(8,128)(2,1)S(1)}, bf16[8,32,512]{2,1,0:T(8,128)(2,1)S(1)}, u32[]{:S(2)}, u32[]{:S(2)}) collective-permute-start(bf16[8,32,512]{2,1,0:T(8,128)(2,1)S(1)} %bitcast.118), channel_id=1, source_target_pairs={{0,8},{8,16},{16,24},{24,32},{32,40},{40,48},{48,56},{56,64},{64,7... | collective-permute-start | bytes 786440 | tf_op jit(solution)/shard_map/ppermute | solution.py:10
  154.5 9.4 %collective-permute-start.6 = (bf16[8,32,512]{2,1,0:T(8,128)(2,1)S(1)}, bf16[8,32,512]{2,1,0:T(8,128)(2,1)S(1)}, u32[]{:S(2)}, u32[]{:S(2)}) collective-permute-start(bf16[8,32,512]{2,1,0:T(8,128)(2,1)S(1)} %bitcast.112), channel_id=1, source_target_pairs={{8,0},{16,8},{24,16},{32,24},{40,32},{48,40},{56,48},{64,56},{72,6... | collective-permute-start | bytes 786440 | tf_op jit(solution)/shard_map/ppermute | solution.py:10
  164.9 7.1 %copy-start.26 = (s32[1,3,8,32]{3,2,1,0:T(8,128)S(1)}, s32[1,3,8,32]{3,2,1,0:T(8,128)}, u32[]{:S(2)}) copy-start(s32[1,3,8,32]{3,2,1,0:T(8,128)} %param.24) | copy-start | bytes 9220
  164.9 7.2 %copy-start.8 = (bf16[512,512]{1,0:T(8,128)(2,1)S(1)}, bf16[512,512]{1,0:T(8,128)(2,1)}, u32[]{:S(2)}) copy-start(bf16[512,512]{1,0:T(8,128)(2,1)} %param.22) | copy-start | bytes 1572868
  164.9 24.3 %all-to-all-start.3 = ((bf16[3,8,32,512]{3,2,0,1:T(8,128)(2,1)}), bf16[3,8,32,512]{3,2,0,1:T(8,128)(2,1)}, u32[]{:S(2)}, u32[]{:S(2)}) async-start(bf16[3,8,32,512]{3,2,0,1:T(8,128)(2,1)} %rev.9), calls=%async_computation.3 | async-start | bytes 1572864 | tf_op jit(solution)/shard_map/all_to_all | solution.py:35
  189.2 9.2 %copy-start.1 = (f32[128,512]{1,0:T(8,128)}, f32[128,512]{1,0:T(8,128)S(1)}, u32[]{:S(2)}) copy-start(f32[128,512]{1,0:T(8,128)S(1)} %scatter_fusion.1) | copy-start | bytes 786436
  (22 other events, 57.1 us)
Sparse Core Ops, SparseCore 0:
  148.6 167.6 all-reduce.2
where the time goes:
time: 333 us; the launch traced here: 332 us
  waiting for transfers between devices  167 us (50%)
  starting transfers between devices  46.6 us (14%)
  other arithmetic  39.3 us (12%)
  local copies, waits for them, and re-layouts  37.7 us (11%)
  matrix products  27.3 us (8%)
  between operations  14.6 us (4%)
    psum x1, waiting for transfers between devices, per_device(): lax.psum((grad_enc_send * factor, grad_enc_recv * factor, grad_enc_out *...  118 us
    ppermute x8, waiting for transfers between devices, from_behind(): return lax.ppermute(block, axis, route)  26 us
    all_to_all x4, starting transfers between devices, patch_move(): lax.all_to_all(rows, 'patch', split_axis=1, concat_axis=1, tiled=True)  25.5 us
    all_to_all x4, waiting for transfers between devices, patch_move(): lax.all_to_all(rows, 'patch', split_axis=1, concat_axis=1, tiled=True)  22.7 us
    ppermute x8, starting transfers between devices, from_behind(): return lax.ppermute(block, axis, route)  21.1 us
    dot_general x6, matrix products, outer_sum(): lax.dot_general(left, right, (((0,), (0,)), ((), ())), preferred_element_...  12.5 us
    unnamed x74, local copies, waits for them, and re-layouts  11.5 us
    scatter-add x1, other arithmetic, per_device(): jax.ops.segment_sum(enc_msg, enc_target, mesh_nodes)  9.2 us
  transfers between devices with their start and end apart: 13, of which 12 were waited for; matrix products, arithmetic and copies ran while one was open for 14% of the time, Pallas kernels for 0%

commit v1 on v0

--- a/solution.py
+++ b/solution.py
@@ -1,13 +1,198 @@
+import functools
+import itertools
+
 import jax
 import jax.numpy as jnp
 from jax import lax
+from jax.experimental import pallas as pl
+from jax.experimental.pallas import tpu as pltpu
 from jax.sharding import PartitionSpec as P
 
-
-def from_behind(block, axis, distance):
-    devices = range(lax.axis_size(axis))
-    route = [(i - distance, i) for i in devices if i - distance in devices]
-    return lax.ppermute(block, axis, route)
+MESH = pl.DeviceIdType.MESH
+NB, NP = 16, 8
+SIZES = {"z": 4, "x": 4, "y": 4, "c": 2}
+
+def position():
+    b, p = lax.axis_index("band"), lax.axis_index("patch")
+    return {"z": b // 4, "x": lax.rem(b, 4), "y": p // 2, "c": lax.rem(p, 2)}
+
+def device(pos):
+    return (pos["z"] * 4 + pos["x"], pos["y"] * 2 + pos["c"])
+
+def offsets(axes):
+    return [d for d in itertools.product(*[range(SIZES[a]) for a in axes]) if any(d)]
+
+def partner(pos, axes, d):
+    new = dict(pos)
+    for a, k in zip(axes, d):
+        new[a] = lax.rem(pos[a] + k, SIZES[a])
+    return new
+
+def index(pos, axes):
+    i = 0
+    for a in axes:
+        i = i * SIZES[a] + pos[a]
+    return i
+
+def geometry(plan):
+    R = C = 512
+    out = []
+    for axes in plan:
+        g = 1
+        for a in axes:
+            g *= SIZES[a]
+        rs = min(g, R // 16)
+        cs = g // rs
+        out.append((axes, g, (R, C), (R // rs, C // cs), cs))
+        R, C = R // rs, C // cs
+    return out
+
+def scratch_for(plan):
+    shapes = []
+    for axes, g, (R, C), (pr, pc), cs in geometry(plan):
+        shapes += [pltpu.VMEM((pr, pc), jnp.float32), pltpu.VMEM((pr, pc), jnp.bfloat16), pltpu.VMEM((g - 1, pr, pc), jnp.bfloat16)]
+    return shapes
+
+def piece(k, cs, pr, pc):
+    r = (k // cs) * pr
+    c = lax.rem(k, cs) * pc if cs > 1 else 0
+    r = pl.multiple_of(r, 16) if not isinstance(r, int) else r
+    if cs > 1: c = pl.multiple_of(c, 128)
+    return r, c
+
+def rs_send(pos, geo, s, srcb, recv, ssem, rsem):
+    axes, g, _, (pr, pc), cs = geo[s]
+    for n, d in enumerate(offsets(axes)):
+        to = partner(pos, axes, d)
+        r, c = piece(index(to, axes), cs, pr, pc)
+        pltpu.make_async_remote_copy(srcb.at[pl.ds(r, pr), pl.ds(c, pc)], recv.at[n], ssem, rsem, device_id=device(to), device_id_type=MESH).start()
+
+def wait_bytes(ref, sem):
+    pltpu.make_async_copy(ref, ref, sem).wait()
+
+def rs_sum(pos, geo, s, cur, recv, rsem):
+    axes, g, _, (pr, pc), cs = geo[s]
+    wait_bytes(recv, rsem)
+    r, c = piece(index(pos, axes), cs, pr, pc)
+    total = cur[pl.ds(r, pr), pl.ds(c, pc)]
+    for n in range(g - 1):
+        total = total + recv[n].astype(jnp.float32)
+    return total
+
+def regions(pos, geo):
+    r0 = c0 = 0
+    out = [(0, 0)]
+    for axes, g, _, (pr, pc), cs in geo:
+        r, c = piece(index(pos, axes), cs, pr, pc)
+        r0, c0 = r0 + r, c0 + c
+        out.append((pl.multiple_of(r0, 16), pl.multiple_of(c0, 128)))
+    return out
+
+def ag_send(pos, geo, regs, s, out, ssem, rsem):
+    axes, g, _, (pr, pc), cs = geo[s]
+    r, c = regs[s + 1]
+    view = out.at[pl.ds(r, pr), pl.ds(c, pc)]
+    for n, d in enumerate(offsets(axes)):
+        to = partner(pos, axes, d)
+        pltpu.make_async_remote_copy(view, view, ssem, rsem, device_id=device(to), device_id_type=MESH).start()
+
+
+def sum_kernel(plans, *refs):
+    T = len(plans)
+    acc, out = refs[:T], refs[T]
+    refs = refs[T + 1:]
+    sbf = refs[0]; refs = refs[1:]
+    geos = [geometry(p) for p in plans]
+    S = len(plans[0])
+    scr = []
+    for t in range(T):
+        scr.append([refs[3 * s:3 * s + 3] for s in range(S)]); refs = refs[3 * S:]
+    ssem, rsem = refs
+    pos = position()
+    seen = []
+    for p in plans:
+        for axes in p:
+            for d in offsets(axes):
+                full = tuple(dict(zip(axes, d)).get(a, 0) for a in "zxyc")
+                if full not in seen: seen.append(full)
+    bar = pltpu.get_barrier_semaphore()
+    for d in seen:
+        pl.semaphore_signal(bar, inc=1, device_id=device(partner(pos, "zxyc", d)), device_id_type=MESH)
+    pl.semaphore_wait(bar, len(seen))
+    for t in range(T):
+        sbf[t] = acc[t][...].astype(jnp.bfloat16)
+        rs_send(pos, geos[t], 0, sbf.at[t], scr[t][0][2], ssem.at[t, 0], rsem.at[t, 0])
+    for s in range(S):
+        for t in range(T):
+            cur = acc[t] if s == 0 else scr[t][s - 1][0]
+            total = rs_sum(pos, geos[t], s, cur, scr[t][s][2], rsem.at[t, s])
+            if s < S - 1:
+                scr[t][s][0][...] = total
+                scr[t][s][1][...] = total.astype(jnp.bfloat16)
+                rs_send(pos, geos[t], s + 1, scr[t][s][1], scr[t][s + 1][2], ssem.at[t, s + 1], rsem.at[t, s + 1])
+            else:
+                regs = regions(pos, geos[t])
+                pr, pc = geos[t][s][3]
+                r, c = regs[-1]
+                out[t, pl.ds(r, pr), pl.ds(c, pc)] = total.astype(jnp.bfloat16)
+                ag_send(pos, geos[t], regs, s, out.at[t], ssem.at[t, S + s], rsem.at[t, S + s])
+    for s in reversed(range(S)):
+        for t in range(T):
+            wait_bytes(scr[t][s][2], rsem.at[t, S + s])
+            if s > 0:
+                ag_send(pos, geos[t], regions(pos, geos[t]), s - 1, out.at[t], ssem.at[t, S + s - 1], rsem.at[t, S + s - 1])
+    for t in range(T):
+        for s in range(S):
+            wait_bytes(scr[t][s][2], ssem.at[t, s])
+            wait_bytes(scr[t][s][2], ssem.at[t, S + s])
+
+def sum_over_devices(mats, plans, cid, name):
+    T, S = len(plans), len(plans[0])
+    scratch = [pltpu.VMEM((T, 512, 512), jnp.bfloat16)]
+    for p in plans: scratch += scratch_for(p)
+    scratch += [pltpu.SemaphoreType.DMA((T, 2 * S))] * 2
+    return pl.pallas_call(functools.partial(sum_kernel, plans),
+        out_shape=jax.ShapeDtypeStruct((T, 512, 512), jnp.bfloat16),
+        in_specs=[pl.BlockSpec(memory_space=pltpu.VMEM)] * T, out_specs=pl.BlockSpec(memory_space=pltpu.VMEM),
+        scratch_shapes=scratch, compiler_params=pltpu.CompilerParams(collective_id=cid, has_side_effects=True, vmem_limit_bytes=40 << 20), name=name)(*mats)
+
+
+def exchange_kernel(sign, send, recv, send_sem, recv_sem):
+    b, p = lax.axis_index("band"), lax.axis_index("patch")
+    routes = [(o, j) for j in (4, 3, 5, 2, 6, 1, 7, 0) for o in (0, 2, 1)]
+    bar = pltpu.get_barrier_semaphore()
+    for o, j in routes:
+        if (o, j) != (1, 0):
+            tb = lax.rem(b + sign * (o - 1) + NB, NB)
+            pl.semaphore_signal(bar, inc=1, device_id=(tb, lax.rem(p + j, NP)), device_id_type=MESH)
+    pl.semaphore_wait(bar, 23)
+    for o, j in routes:
+        q = lax.rem(p + j, NP)
+        tb = lax.rem(b + sign * (o - 1) + NB, NB)
+        if (o, j) == (1, 0):
+            pltpu.make_async_copy(send.at[o, q], recv.at[o, p], recv_sem.at[o]).start()
+        else:
+            pltpu.make_async_remote_copy(
+                send.at[o, q], recv.at[o, p], send_sem.at[o], recv_sem.at[o],
+                device_id=(tb, q), device_id_type=MESH,
+            ).start()
+    for o in range(3):
+        wait_bytes(recv.at[o], recv_sem.at[o])
+    for o in range(3):
+        wait_bytes(send.at[o] if o != 1 else send.at[o, pl.ds(0, 7)], send_sem.at[o])
+
+
+def exchange(rows, sign, cid):
+    return pl.pallas_call(
+        functools.partial(exchange_kernel, sign),
+        out_shape=jax.ShapeDtypeStruct(rows.shape, rows.dtype),
+        in_specs=[pl.BlockSpec(memory_space=pltpu.VMEM)],
+        out_specs=pl.BlockSpec(memory_space=pltpu.VMEM),
+        scratch_shapes=[pltpu.SemaphoreType.DMA((3,)), pltpu.SemaphoreType.DMA((3,))],
+        compiler_params=pltpu.CompilerParams(
+            collective_id=cid, has_side_effects=True, vmem_limit_bytes=16 << 20
+        ),
+    )(rows)
 
 
 def product(left, right):
@@ -29,32 +214,6 @@
 def silu_slope(value):
     sigma = jax.nn.sigmoid(value)
     return sigma * (1.0 + value * (1.0 - sigma))
-
-
-def patch_move(rows):
-    return lax.all_to_all(rows, "patch", split_axis=1, concat_axis=1, tiled=True)
-
-
-def band_forward(rows):
-    pieces = []
-    for offset in range(3):
-        if offset == 1:
-            pieces.append(rows[1])
-        else:
-            pieces.append(from_behind(rows[offset], "band", offset - 1))
-    return jnp.stack(pieces)
-
-
-def band_backward(rows):
-    return band_forward(rows[::-1])[::-1]
-
-
-def send_out(rows):
-    return band_forward(patch_move(rows))
-
-
-def send_back(rows):
-    return patch_move(band_backward(rows))
 
 
 def per_device(
@@ -89,7 +248,7 @@
     enc_target = enc_receiver[0].reshape(flat)
     dec_source = dec_sender[0].reshape(flat)
     dec_target = dec_receiver[0].reshape(flat)
-    sender_rows = send_out(grid_latent[enc_sender[0]]).reshape(flat, width)
+    sender_rows = exchange(grid_latent[enc_sender[0]], 1, 0).reshape(flat, width)
     receiver_rows = mesh_latent[enc_target]
     enc_pre = product(sender_rows, enc_w_send) + product(receiver_rows, enc_w_recv)
     enc_act = jax.nn.silu(enc_pre).astype(jnp.bfloat16)
@@ -97,7 +256,7 @@
     mesh_new = (
         mesh_latent.astype(jnp.float32) + jax.ops.segment_sum(enc_msg, enc_target, mesh_nodes)
     ).astype(jnp.bfloat16)
-    mesh_rows = send_out(mesh_new[dec_sender[0]]).reshape(flat, width)
+    mesh_rows = exchange(mesh_new[dec_sender[0]], 1, 1).reshape(flat, width)
     grid_rows = grid_latent[dec_target]
     dec_pre = product(mesh_rows, dec_w_send) + product(grid_rows, dec_w_recv)
     dec_act = jax.nn.silu(dec_pre).astype(jnp.bfloat16)
@@ -106,7 +265,7 @@
     dec_dsend = (
         product_back(dec_dpre, dec_w_send).astype(jnp.bfloat16).reshape(3, patches, slots, width)
     )
-    mesh_return = send_back(dec_dsend).reshape(flat, width)
+    mesh_return = exchange(dec_dsend, -1, 2).reshape(flat, width)
     grid_from_decoder = jax.ops.segment_sum(
         product_back(dec_dpre, dec_w_recv), dec_target, grid_nodes
     )
@@ -121,7 +280,7 @@
     enc_dsend = (
         product_back(enc_dpre, enc_w_send).astype(jnp.bfloat16).reshape(3, patches, slots, width)
     )
-    grid_return = send_back(enc_dsend).reshape(flat, width)
+    grid_return = exchange(enc_dsend, -1, 3).reshape(flat, width)
     mesh_grad = mesh_grad_new + jax.ops.segment_sum(
         product_back(enc_dpre, enc_w_recv), enc_target, mesh_nodes
     )
@@ -133,17 +292,9 @@
         grid_return.astype(jnp.float32), enc_source, grid_nodes
     )
     factor = float(devices * 3 * patches * slots) ** (-0.5)
-    totals = lax.psum(
-        (
-            grad_enc_send * factor,
-            grad_enc_recv * factor,
-            grad_enc_out * factor,
-            grad_dec_send * factor,
-            grad_dec_recv * factor,
-            grad_dec_out * factor,
-        ),
-        ("band", "patch"),
-    )
+    plans = [("c", "y", "xz"), ("c", "x", "zy"), ("c", "z", "yx")] * 2
+    grads = [grad_enc_send, grad_enc_recv, grad_enc_out, grad_dec_send, grad_dec_recv, grad_dec_out]
+    totals = sum_over_devices(grads, plans, 4, "gradients").astype(jnp.float32) * factor
     return (grid_grad, mesh_grad, totals[0], totals[1], totals[2], totals[3], totals[4], totals[5])
 
 

time: 333 us -> 196 us (0.59)
  waiting for transfers between devices: 167 us -> 0 us
  Pallas kernels: 0 us -> 94.5 us
  starting transfers between devices: 46.6 us -> 0 us
  between operations: 14.6 us -> 1.15 us
  other arithmetic: 39.3 us -> 48.5 us
  matrix products: 27.3 us -> 18.8 us
  local copies, waits for them, and re-layouts: 37.7 us -> 31.7 us
    psum x1 -> x0, waiting for transfers between devices: 118 us -> none  [per_device(): lax.psum((grad_enc_send * factor, grad_enc_recv * factor, grad_enc_out *...]
    pallas_call x0 -> x5, Pallas kernels: none -> 94.5 us  [the longest x4 62.5 us: exchange(): pl.pallas_call(functools.partial(exchange_kernel, sign), out_shape=jax.Sh...]
    ppermute x8 -> x0, waiting for transfers between devices: 26 us -> none  [from_behind(): return lax.ppermute(block, axis, route)]
    all_to_all x4 -> x0, starting transfers between devices: 25.5 us -> none  [patch_move(): lax.all_to_all(rows, 'patch', split_axis=1, concat_axis=1, tiled=True)]
    all_to_all x4 -> x0, waiting for transfers between devices: 22.7 us -> none  [patch_move(): lax.all_to_all(rows, 'patch', split_axis=1, concat_axis=1, tiled=True)]
    ppermute x8 -> x0, starting transfers between devices: 21.1 us -> none  [from_behind(): return lax.ppermute(block, axis, route)]
    dot_general x6, matrix products: 12.5 us -> 4.94 us  [outer_sum(): lax.dot_general(left, right, (((0,), (0,)), ((), ())), preferred_element_...]
    unnamed x74 -> x56, local copies, waits for them, and re-layouts: 11.5 us -> 5.97 us
  transfers between devices with their start and end apart: 13 -> 0, of which waited for: 12 -> 0; matrix products, arithmetic and copies ran while one was open for 14% -> 0% of each run, Pallas kernels for 0% -> 0%
where the time goes in v1:
time: 196 us; the launch traced here: 195 us
  Pallas kernels  94.5 us (48%)
  other arithmetic  48.5 us (25%)
  local copies, waits for them, and re-layouts  31.7 us (16%)
  matrix products  18.8 us (10%)
    pallas_call x4, Pallas kernels, exchange(): pl.pallas_call(functools.partial(exchange_kernel, sign), out_shape=jax.Sh...  62.5 us
    pallas_call x1, Pallas kernels, sum_over_devices(): pl.pallas_call(functools.partial(sum_kernel, plans), out_shape=jax.ShapeD...  32 us
    scatter-add x1, other arithmetic, per_device(): jax.ops.segment_sum(enc_msg, enc_target, mesh_nodes)  9.38 us
    dot_general x6, matrix products, product_back(): lax.dot_general(left, weight, (((1,), (1,)), ((), ())), preferred_element...  8.51 us
    scatter-add x1, other arithmetic, per_device(): jax.ops.segment_sum(mesh_return.astype(jnp.float32), dec_source, mesh_nodes)  7.87 us
    scatter-add x1, other arithmetic, per_device(): jax.ops.segment_sum(product_back(enc_dpre, enc_w_recv), enc_target, mesh_...  7.68 us
    scatter-add x1, other arithmetic, per_device(): jax.ops.segment_sum(product_back(dec_dpre, dec_w_recv), dec_target, grid_...  7.47 us
    scatter-add x1, other arithmetic, per_device(): jax.ops.segment_sum(grid_return.astype(jnp.float32), enc_source, grid_nodes)  7.1 us

profile of v1, /device:TPU:1, one launch (start us, length us, event | category | flops | bytes accessed | tf_op | source)
XLA Modules:
  0.0 194.7 jit_solution(17782122001316626915)
XLA Ops:
  10.3 1.8 convert_element_type.45
  12.1 2.7 %gather_fusion.1 = bf16[768,512]{1,0:T(8,128)(2,1)S(1)} fusion(bf16[256,512]{1,0:T(8,128)(2,1)S(1)} %copy-done.6, s32[1024]{0:T(1024)S(1)} %pad_clamp_fusion.2), kind=kCustom, calls=%fused_computation.1 | custom fusion | bytes 1575936 | tf_op jit(solution)/shard_map/gather | solution.py:251
  14.8 18.8 %shard_map.206 = bf16[3,8,32,512]{3,2,1,0:T(8,128)(2,1)S(1)} custom-call(bf16[3,8,32,512]{3,2,1,0:T(8,128)(2,1)S(1)} %bitcast.86), custom_call_target="tpu_custom_call" | custom-call | tf_op jit(solution)/shard_map/pallas_call | solution.py:186
  33.6 2.7 %gather_fusion.4 = bf16[768,512]{1,0:T(8,128)(2,1)S(1)} fusion(bf16[256,512]{1,0:T(8,128)(2,1)S(1)} %copy-done.6, s32[1024]{0:T(1024)S(1)} %pad_clamp_fusion.3), kind=kCustom, calls=%fused_computation.4 | custom fusion | bytes 1575936 | tf_op jit(solution)/shard_map/gather | solution.py:260
  36.3 3.3 %gather_fusion = bf16[768,512]{1,0:T(8,128)(2,1)} fusion(bf16[256,512]{1,0:T(8,128)(2,1)S(1)} %copy-done.9, s32[1024]{0:T(1024)S(1)} %pad_clamp_fusion.3), kind=kCustom, calls=%fused_computation | custom fusion | bytes 1575936 | tf_op jit(solution)/shard_map/gather | solution.py:263
  39.7 2.7 %gather_fusion.2 = bf16[768,512]{1,0:T(8,128)(2,1)S(1)} fusion(bf16[128,512]{1,0:T(8,128)(2,1)S(1)} %copy-done.8, s32[1024]{0:T(1024)S(1)} %pad_clamp_fusion.1), kind=kCustom, calls=%fused_computation.2 | custom fusion | bytes 1575936 | tf_op jit(solution)/shard_map/gather | solution.py:252
  42.4 1.9 fusion.20
  46.0 1.8 fusion.19
  47.8 9.4 %scatter_custom_fusion = f32[128,512]{1,0:T(8,128)S(1)} fusion(f32[128,512]{1,0:T(8,128)S(1)} %convert_element_type.46, s32[768]{0:T(1024)S(1)} %reshape.234, f32[768,512]{1,0:T(8,128)} %fusion.19, f32[]{:T(128)} %constant.12.clone.1, pred[768]{0:T(1024)(128)(4,1)S(1)} %lt.96), kind=kCustom, calls=%fused_computation.20 | custom fusion | flops 786432 | bytes 1836036 | tf_op jit(solution)/shard_map/scatter-add | solution.py:257
  57.2 2.7 %gather_fusion.3 = bf16[768,512]{1,0:T(8,128)(2,1)S(1)} fusion(bf16[128,512]{1,0:T(8,128)(2,1)S(1)} %convert_element_type.48, s32[1024]{0:T(1024)S(1)} %pad_clamp_fusion), kind=kCustom, calls=%fused_computation.3 | custom fusion | bytes 1575936 | tf_op jit(solution)/shard_map/gather | solution.py:259
  59.9 14.7 %shard_map.207 = bf16[3,8,32,512]{3,2,1,0:T(8,128)(2,1)S(1)} custom-call(bf16[3,8,32,512]{3,2,1,0:T(8,128)(2,1)S(1)} %bitcast.85), custom_call_target="tpu_custom_call" | custom-call | tf_op jit(solution)/shard_map/pallas_call | solution.py:186
  77.9 1.8 fusion.7.refs_5_
  81.5 14.8 %shard_map.208 = bf16[3,8,32,512]{3,2,1,0:T(8,128)(2,1)S(1)} custom-call(bf16[3,8,32,512]{3,2,1,0:T(8,128)(2,1)S(1)} %bitcast.87), custom_call_target="tpu_custom_call" | custom-call | tf_op jit(solution)/shard_map/pallas_call | solution.py:186
  97.1 7.9 %scatter_custom_fusion.2 = f32[128,512]{1,0:T(8,128)} fusion(s32[768]{0:T(1024)S(1)} %reshape.250, bf16[768,512]{1,0:T(8,128)(2,1)} %bitcast.84, f32[]{:T(128)} %constant.12.clone.1), kind=kCustom, calls=%fused_computation.14 | custom fusion | flops 786432 | bytes 1048580 | tf_op jit(solution)/shard_map/scatter-add | solution.py:275
  106.0 3.3 %gather_fusion.5 = bf16[768,512]{1,0:T(8,128)(2,1)} fusion(bf16[128,512]{1,0:T(8,128)(2,1)S(1)} %convert_element_type.53, s32[1024]{0:T(1024)S(1)} %pad_clamp_fusion.1), kind=kCustom, calls=%fused_computation.5 | custom fusion | bytes 1575936 | tf_op jit(solution)/shard_map/gather | solution.py:277
  109.3 2.9 %multiply_convert_fusion.1 = bf16[768,512]{1,0:T(8,128)(2,1)S(1)} fusion(f32[768,512]{1,0:T(8,128)} %copy-done.20, bf16[512,512]{1,0:T(8,128)(2,1)} %param.20, bf16[768,512]{1,0:T(8,128)(2,1)} %gather_fusion.5, pred[768]{0:T(1024)(128)(4,1)S(1)} %lt.96), kind=kOutput, calls=%fused_computation.17 | convolution fusion | flops 406585344 | bytes 3670784 | tf_op jit(solution)/shard_map/dot_general | solution.py:203
  115.5 32.0 %gradients.1 = bf16[6,512,512]{2,1,0:T(8,128)(2,1)S(1)} custom-call(f32[512,512]{1,0:T(8,128)S(1)} %fusion.24.refs_0_, f32[512,512]{1,0:T(8,128)S(1)} %fusion.25.refs_1_, f32[512,512]{1,0:T(8,128)S(1)} %fusion.9.refs_2_, f32[512,512]{1,0:T(8,128)S(1)} %fusion.26.refs_3_, f32[512,512]{1,0:T(8,128)S(1)} %fusion.27.refs_4_, f32[512,512]{1,0:T(8,128)S(1)} %copy-done.3), custom_call_target="tpu_custom_call" | custom-call | tf_op jit(solution)/shard_map/gradients/pallas_call | solution.py:154
  148.1 14.2 %shard_map.209 = bf16[3,8,32,512]{3,2,1,0:T(8,128)(2,1)S(1)} custom-call(bf16[3,8,32,512]{3,2,1,0:T(8,128)(2,1)S(1)} %bitcast.88), custom_call_target="tpu_custom_call" | custom-call | tf_op jit(solution)/shard_map/pallas_call | solution.py:186
  162.4 7.1 %scatter_custom_fusion.3 = f32[256,512]{1,0:T(8,128)S(1)} fusion(s32[768]{0:T(1024)} %reshape.258, bf16[768,512]{1,0:T(8,128)(2,1)S(1)} %bitcast.83, f32[]{:T(128)} %constant.12.clone.1), kind=kCustom, calls=%fused_computation.12 | custom fusion | flops 786432 | bytes 1311232 | tf_op jit(solution)/shard_map/scatter-add | solution.py:291
  169.5 1.8 fusion.23
  171.3 7.7 %scatter_fusion.1 = f32[128,512]{1,0:T(8,128)S(1)} fusion(f32[128,512]{1,0:T(8,128)S(1)} %copy-done.4, s32[768]{0:T(1024)S(1)} %reshape.234, f32[768,512]{1,0:T(8,128)} %fusion.23), kind=kCustom, calls=%fused_computation.10 | custom fusion | flops 393216 | bytes 4721664 | tf_op jit(solution)/shard_map/scatter-add | solution.py:284
  180.8 7.5 %scatter_fusion = f32[256,512]{1,0:T(8,128)S(1)} fusion(f32[256,512]{1,0:T(8,128)S(1)} %copy-done.7, s32[768]{0:T(1024)S(1)} %reshape.242, f32[768,512]{1,0:T(8,128)} %fusion.22), kind=kCustom, calls=%fused_computation.7 | custom fusion | flops 393216 | bytes 4721664 | tf_op jit(solution)/shard_map/scatter-add | solution.py:269
  189.1 2.8 %convert_multiply_fusion = f32[6,512,512]{2,1,0:T(8,128)S(1)} fusion(bf16[6,512,512]{2,1,0:T(8,128)(2,1)} %copy-done.1), kind=kLoop, calls=%fused_computation.11 | loop fusion | flops 3145728 | bytes 9437184 | tf_op jit(solution)/shard_map/mul | solution.py:297
  192.0 2.7 %slice_bitcast_fusion = (f32[512,512]{1,0:T(8,128)}, f32[512,512]{1,0:T(8,128)}, f32[512,512]{1,0:T(8,128)}, f32[512,512]{1,0:T(8,128)}, f32[512,512]{1,0:T(8,128)}, /*index=5*/f32[512,512]{1,0:T(8,128)}) fusion(f32[6,512,512]{2,1,0:T(8,128)S(1)} %convert_multiply_fusion), kind=kLoop, calls=%fused_computation.28 | loop fusion | bytes 12582912 | tf_op jit(solution)/shard_map/squeeze | solution.py:298
  (92 shorter events, 24.8 us)
Async XLA Ops:
  0.6 74.0 %copy-start = (bf16[512,512]{1,0:T(8,128)(2,1)S(1)}, bf16[512,512]{1,0:T(8,128)(2,1)}, u32[]{:S(2)}) copy-start(bf16[512,512]{1,0:T(8,128)(2,1)} %param.21) | copy-start | bytes 1572868
  0.6 11.5 %copy-start.6 = (bf16[256,512]{1,0:T(8,128)(2,1)S(1)}, bf16[256,512]{1,0:T(8,128)(2,1)}, u32[]{:S(2)}) copy-start(bf16[256,512]{1,0:T(8,128)(2,1)} %param.15) | copy-start | bytes 786436
  33.6 2.7 %copy-start.9 = (bf16[256,512]{1,0:T(8,128)(2,1)S(1)}, bf16[256,512]{1,0:T(8,128)(2,1)}, u32[]{:S(2)}) copy-start(bf16[256,512]{1,0:T(8,128)(2,1)} %param.17) | copy-start | bytes 786436
  36.3 3.3 %copy-start.8 = (bf16[128,512]{1,0:T(8,128)(2,1)S(1)}, bf16[128,512]{1,0:T(8,128)(2,1)}, u32[]{:S(2)}) copy-start(bf16[128,512]{1,0:T(8,128)(2,1)} %param.16) | copy-start | bytes 393220
  42.3 2.5 %copy-start.12 = (bf16[768,512]{1,0:T(8,128)(2,1)}, bf16[768,512]{1,0:T(8,128)(2,1)S(1)}, u32[]{:S(2)}) copy-start(bf16[768,512]{1,0:T(8,128)(2,1)S(1)} %gather_fusion.2) | copy-start | bytes 2359300
  42.4 1.9 copy-start.16
  44.3 1.7 copy-start.26
  44.9 1.1 copy-start.20
  75.6 1.3 copy-start.25
  77.9 3.0 %copy-start.10 = (bf16[768,512]{1,0:T(8,128)(2,1)}, bf16[768,512]{1,0:T(8,128)(2,1)S(1)}, u32[]{:S(2)}) copy-start(bf16[768,512]{1,0:T(8,128)(2,1)S(1)} %multiply_convert_fusion.2) | copy-start | bytes 2359300
  109.3 2.9 %copy-start.21 = (f32[768,512]{1,0:T(8,128)S(1)}, f32[768,512]{1,0:T(8,128)}, u32[]{:S(2)}) copy-start(f32[768,512]{1,0:T(8,128)} %copy-done.20) | copy-start | bytes 4718596
  109.3 2.9 %copy-start.23 = (bf16[768,512]{1,0:T(8,128)(2,1)S(1)}, bf16[768,512]{1,0:T(8,128)(2,1)}, u32[]{:S(2)}) copy-start(bf16[768,512]{1,0:T(8,128)(2,1)} %gather_fusion.5) | copy-start | bytes 2359300
  112.2 35.3 %copy-start.14 = (bf16[768,512]{1,0:T(8,128)(2,1)}, bf16[768,512]{1,0:T(8,128)(2,1)S(1)}, u32[]{:S(2)}) copy-start(bf16[768,512]{1,0:T(8,128)(2,1)S(1)} %multiply_convert_fusion.1) | copy-start | bytes 2359300
  112.2 1.4 copy-start.13
  114.2 1.2 copy-start.3
  115.4 32.0 %copy-start.24 = (bf16[512,512]{1,0:T(8,128)(2,1)S(1)}, bf16[512,512]{1,0:T(8,128)(2,1)}, u32[]{:S(2)}) copy-start(bf16[512,512]{1,0:T(8,128)(2,1)} %param.18) | copy-start | bytes 1572868
  147.5 14.9 %copy-start.1 = (bf16[6,512,512]{2,1,0:T(8,128)(2,1)}, bf16[6,512,512]{2,1,0:T(8,128)(2,1)S(1)}, u32[]{:S(2)}) copy-start(bf16[6,512,512]{2,1,0:T(8,128)(2,1)S(1)} %gradients.1) | copy-start | bytes 9437188
  148.1 21.4 %copy-start.15 = (bf16[768,512]{1,0:T(8,128)(2,1)S(1)}, bf16[768,512]{1,0:T(8,128)(2,1)}, u32[]{:S(2)}) copy-start(bf16[768,512]{1,0:T(8,128)(2,1)} %copy-done.14) | copy-start | bytes 2359300
  148.1 21.4 %copy-start.17 = (bf16[512,512]{1,0:T(8,128)(2,1)S(1)}, bf16[512,512]{1,0:T(8,128)(2,1)}, u32[]{:S(2)}) copy-start(bf16[512,512]{1,0:T(8,128)(2,1)} %param.19) | copy-start | bytes 1572868
  169.5 1.8 copy-start.4
  171.3 7.7 %copy-start.11 = (bf16[768,512]{1,0:T(8,128)(2,1)S(1)}, bf16[768,512]{1,0:T(8,128)(2,1)}, u32[]{:S(2)}) copy-start(bf16[768,512]{1,0:T(8,128)(2,1)} %copy-done.10) | copy-start | bytes 2359300
  171.3 7.7 %copy-start.19 = (bf16[512,512]{1,0:T(8,128)(2,1)S(1)}, bf16[512,512]{1,0:T(8,128)(2,1)}, u32[]{:S(2)}) copy-start(bf16[512,512]{1,0:T(8,128)(2,1)} %param.22) | copy-start | bytes 1572868
  179.0 9.3 %copy-start.5 = (f32[128,512]{1,0:T(8,128)}, f32[128,512]{1,0:T(8,128)S(1)}, u32[]{:S(2)}) copy-start(f32[128,512]{1,0:T(8,128)S(1)} %scatter_fusion.1) | copy-start | bytes 786436
  179.0 1.8 copy-start.7
  (3 other events, 3.1 us)

commit v2 on v1

v2 whole, which is shorter than its diff:
```python
import functools
import itertools

import jax
import jax.numpy as jnp
from jax import lax
from jax.experimental import pallas as pl
from jax.experimental.pallas import tpu as pltpu
from jax.sharding import PartitionSpec as P


MESH = pl.DeviceIdType.MESH
NB, NP = 16, 8
SIZES = {"z": 4, "x": 4, "y": 4, "c": 2}

def position():
    b, p = lax.axis_index("band"), lax.axis_index("patch")
    return {"z": b // 4, "x": lax.rem(b, 4), "y": p // 2, "c": lax.rem(p, 2)}

def device(pos):
    return (pos["z"] * 4 + pos["x"], pos["y"] * 2 + pos["c"])

def offsets(axes):
    return [d for d in itertools.product(*[range(SIZES[a]) for a in axes]) if any(d)]

def partner(pos, axes, d):
    new = dict(pos)
    for a, k in zip(axes, d):
        new[a] = lax.rem(pos[a] + k, SIZES[a])
    return new

def index(pos, axes):
    i = 0
    for a in axes:
        i = i * SIZES[a] + pos[a]
    return i

def geometry(plan):
    R = C = 512
    out = []
    for axes in plan:
        g = 1
        for a in axes:
            g *= SIZES[a]
        rs = min(g, R // 16)
        cs = g // rs
        out.append((axes, g, (R, C), (R // rs, C // cs), cs))
        R, C = R // rs, C // cs
    return out

def scratch_for(plan):
    shapes = []
    for axes, g, (R, C), (pr, pc), cs in geometry(plan):
        shapes += [pltpu.VMEM((pr, pc), jnp.float32), pltpu.VMEM((pr, pc), jnp.bfloat16), pltpu.VMEM((g - 1, pr, pc), jnp.bfloat16)]
    return shapes

def piece(k, cs, pr, pc):
    r = (k // cs) * pr
    c = lax.rem(k, cs) * pc if cs > 1 else 0
    r = pl.multiple_of(r, 16) if not isinstance(r, int) else r
    if cs > 1: c = pl.multiple_of(c, 128)
    return r, c

def rs_send(pos, geo, s, srcb, recv, ssem, rsem):
    axes, g, _, (pr, pc), cs = geo[s]
    for n, d in enumerate(offsets(axes)):
        to = partner(pos, axes, d)
        r, c = piece(index(to, axes), cs, pr, pc)
        pltpu.make_async_remote_copy(srcb.at[pl.ds(r, pr), pl.ds(c, pc)], recv.at[n], ssem, rsem, device_id=device(to), device_id_type=MESH).start()

def wait_bytes(ref, sem):
    pltpu.make_async_copy(ref, ref, sem).wait()

def rs_sum(pos, geo, s, cur, recv, rsem):
    axes, g, _, (pr, pc), cs = geo[s]
    wait_bytes(recv, rsem)
    r, c = piece(index(pos, axes), cs, pr, pc)
    total = cur[pl.ds(r, pr), pl.ds(c, pc)]
    for n in range(g - 1):
        total = total + recv[n].astype(jnp.float32)
    return total

def regions(pos, geo):
    r0 = c0 = 0
    out = [(0, 0)]
    for axes, g, _, (pr, pc), cs in geo:
        r, c = piece(index(pos, axes), cs, pr, pc)
        r0, c0 = r0 + r, c0 + c
        out.append((pl.multiple_of(r0, 16), pl.multiple_of(c0, 128)))
    return out

def ag_send(pos, geo, regs, s, out, ssem, rsem):
    axes, g, _, (pr, pc), cs = geo[s]
    r, c = regs[s + 1]
    view = out.at[pl.ds(r, pr), pl.ds(c, pc)]
    for n, d in enumerate(offsets(axes)):
        to = partner(pos, axes, d)
        pltpu.make_async_remote_copy(view, view, ssem, rsem, device_id=device(to), device_id_type=MESH).start()


F32, BF16 = jnp.float32, jnp.bfloat16
ORDER = (1, 0, 2)
HOPS = (4, 3, 5, 2, 6, 1, 7, 0)
PLANS = [("c", "y", "xz"), ("c", "x", "zy"), ("c", "z", "yx")]
GEO = [geometry(plan) for plan in PLANS]
STAGES = 3
DEC, ENC = 0, 3


def dot(left, right):
    return jnp.dot(left, right, preferred_element_type=F32)


def dot_back(left, weight):
    return lax.dot_general(left, weight, (((1,), (1,)), ((), ())), preferred_element_type=F32)


def outer(left, right):
    return lax.dot_general(left, right, (((0,), (0,)), ((), ())), preferred_element_type=F32)


def split(value):
    high = value.astype(BF16)
    return high, (value - high.astype(F32)).astype(BF16)


def sigmoid(value):
    return 1.0 / (1.0 + jnp.exp(-value))


def chunk(o):
    return pl.ds(o * 256, 256)


def pick(ref, o, rows, count=None):
    columns = jnp.transpose(ref[0, o])
    parts = []
    for q in range(NP):
        column = columns[:, q : q + 1]
        hit = lax.broadcasted_iota(jnp.int32, (32, rows), 1) == column
        if count is not None:
            slot = lax.broadcasted_iota(jnp.int32, (32, rows), 0)
            hit = hit & (slot < count[0, o, q])
        parts.append(jnp.where(hit, 1.0, 0.0).astype(BF16))
    return jnp.concatenate(parts, axis=0)


def edge_send(sign, o, b, p, send, recv, send_sem, recv_sem):
    band = lax.rem(b + sign * (o - 1) + NB, NB)
    for j in HOPS:
        q = lax.rem(p + j, NP)
        src = send.at[o, pl.ds(pl.multiple_of(q * 32, 32), 32)]
        dst = recv.at[o, pl.ds(pl.multiple_of(p * 32, 32), 32)]
        if o == 1 and j == 0:
            pltpu.make_async_copy(src, dst, recv_sem.at[o]).start()
        else:
            pltpu.make_async_remote_copy(
                src, dst, send_sem.at[o], recv_sem.at[o],
                device_id=(band, q), device_id_type=MESH,
            ).start()


def greet(b, p, pos):
    bar = pltpu.get_barrier_semaphore()
    n = 0
    for o in range(3):
        band = lax.rem(b + o - 1 + NB, NB)
        for j in HOPS:
            if (o, j) != (1, 0):
                pl.semaphore_signal(
                    bar, inc=1, device_id=(band, lax.rem(p + j, NP)), device_id_type=MESH
                )
                n += 1
    seen = []
    for plan in PLANS:
        for axes in plan:
            for d in offsets(axes):
                full = tuple(dict(zip(axes, d)).get(a, 0) for a in "zxyc")
                if full not in seen:
                    seen.append(full)
    for d in seen:
        pl.semaphore_signal(
            bar, inc=1, device_id=device(partner(pos, "zxyc", d)), device_id_type=MESH
        )
    return bar, n + len(seen)


class Sum:
    def __init__(self, pos, t, acc, sbf, scr, out, ssem, rsem):
        self.pos, self.geo = pos, GEO[t % 3]
        self.acc, self.sbf, self.out = acc.at[t], sbf.at[t], out[t]
        self.scr = scr[t]
        self.ssem, self.rsem = ssem, rsem
        self.t = t

    def begin(self):
        pos, geo = self.pos, self.geo
        other = pl.ds(pl.multiple_of((1 - pos["c"]) * 256, 256), 256)
        self.sbf[other, :] = self.acc[other, :].astype(BF16)
        rs_send(pos, geo, 0, self.sbf, self.scr[0][2], self.ssem.at[self.t, 0], self.rsem.at[self.t, 0])

    def reduce(self, s):
        pos, geo, scr, t = self.pos, self.geo, self.scr, self.t
        cur = self.acc if s == 0 else scr[s - 1][0]
        total = rs_sum(pos, geo, s, cur, scr[s][2], self.rsem.at[t, s])
        if s < STAGES - 1:
            scr[s][0][...] = total
            scr[s][1][...] = total.astype(BF16)
            rs_send(pos, geo, s + 1, scr[s][1], scr[s + 1][2], self.ssem.at[t, s + 1], self.rsem.at[t, s + 1])
        else:
            pr, pc = geo[s][3]
            r, c = regions(pos, geo)[-1]
            self.out[pl.ds(r, pr), pl.ds(c, pc)] = total.astype(BF16)
            self.spread(s)

    def spread(self, s):
        ag_send(self.pos, self.geo, regions(self.pos, self.geo), s, self.out,
                self.ssem.at[self.t, STAGES + s], self.rsem.at[self.t, STAGES + s])

    def gather(self, s):
        wait_bytes(self.scr[s][2], self.rsem.at[self.t, STAGES + s])
        if s > 0:
            self.spread(s - 1)

    def end(self):
        for s in range(STAGES):
            wait_bytes(self.scr[s][2], self.ssem.at[self.t, s])
            wait_bytes(self.scr[s][2], self.ssem.at[self.t, STAGES + s])


def kernel(
    grid, mesh, cot, w_es, w_er, w_eo, w_ds, w_dr, w_do,
    i_es, i_er, n_e, i_ds, i_dr, n_d,
    grid_out, mesh_out, o0, o1, o2, o3, o4, o5,
    send, recv, oh_es, oh_er, oh_ds, oh_dr, t_es, t_er, t_ds, t_dr,
    enc_pre, dec_pre, dec_back, enc_d, dec_d, acc, sbf, *rest,
):
    scr = []
    for t in range(6):
        n = 9 * t
        scr.append([rest[n + 3 * s : n + 3 * s + 3] for s in range(STAGES)])
    esend, erecv, ssem, rsem = rest[54:]
    outs = [o3, o4, o5, o0, o1, o2]
    b, p = lax.axis_index("band"), lax.axis_index("patch")
    pos = position()
    bar, greeted = greet(b, p, pos)

    def edges(phase, sign, o):
        edge_send(sign, o, b, p, send.at[phase], recv.at[phase], esend.at[phase], erecv.at[phase])

    def arrive(phase, o):
        wait_bytes(recv.at[phase, o], erecv.at[phase, o])

    sums = [Sum(pos, t, acc, sbf, scr, outs, ssem, rsem) for t in range(6)]
    dec_sums, enc_sums = sums[:3], sums[3:]

    for n, o in enumerate(ORDER):
        oh_es[chunk(o), :] = pick(i_es, o, 256)
        send[0, o] = dot(oh_es[chunk(o), :], grid[...]).astype(BF16)
        if n == 0:
            pl.semaphore_wait(bar, greeted)
        edges(0, 1, o)

    for o in range(3):
        oh_er[chunk(o), :] = pick(i_er, o, 128, n_e)
        t_er[:, chunk(o)] = jnp.transpose(oh_er[chunk(o), :])
    high, low = split(dot(mesh[...], w_er[...]))
    for o in range(3):
        enc_pre[chunk(o), :] = dot(oh_er[chunk(o), :], high) + dot(oh_er[chunk(o), :], low)
    for o in range(3):
        oh_ds[chunk(o), :] = pick(i_ds, o, 128)
        t_ds[:, chunk(o)] = jnp.transpose(oh_ds[chunk(o), :])
        oh_dr[chunk(o), :] = pick(i_dr, o, 256, n_d)
        t_dr[:, chunk(o)] = jnp.transpose(oh_dr[chunk(o), :])
        t_es[:, chunk(o)] = jnp.transpose(oh_es[chunk(o), :])
    high, low = split(dot(grid[...], w_dr[...]))
    for o in range(3):
        dec_pre[chunk(o), :] = dot(oh_dr[chunk(o), :], high) + dot(oh_dr[chunk(o), :], low)
    high, low = split(dot_back(cot[...], w_do[...]))
    for o in range(3):
        dec_back[chunk(o), :] = dot(oh_dr[chunk(o), :], high) + dot(oh_dr[chunk(o), :], low)

    enc_sum = None
    for o in ORDER:
        arrive(0, o)
        pre = dot(recv[0, o], w_es[...]) + enc_pre[chunk(o), :]
        enc_pre[chunk(o), :] = pre
        act = (pre * sigmoid(pre)).astype(BF16)
        part = dot(t_er[:, chunk(o)], act)
        enc_sum = part if enc_sum is None else enc_sum + part
    high, low = split(enc_sum)
    mesh_new = (mesh[...].astype(F32) + (dot(high, w_eo[...]) + dot(low, w_eo[...]))).astype(BF16)

    for o in ORDER:
        send[1, o] = dot(oh_ds[chunk(o), :], mesh_new).astype(BF16)
        edges(1, 1, o)
    for o in range(3):
        pre = enc_pre[chunk(o), :]
        sigma = sigmoid(pre)
        enc_pre[chunk(o), :] = sigma * (1.0 + pre * (1.0 - sigma))
    enc_act_sum = high

    act_sum = None
    for o in ORDER:
        arrive(1, o)
        pre = dot(recv[1, o], w_ds[...]) + dec_pre[chunk(o), :]
        sigma = sigmoid(pre)
        slope = sigma * (1.0 + pre * (1.0 - sigma))
        dpre = (dec_back[chunk(o), :] * slope).astype(BF16)
        dec_d[chunk(o), :] = dpre
        send[2, o] = dot_back(dpre, w_ds[...]).astype(BF16)
        edges(2, -1, o)
        part = dot(t_dr[:, chunk(o)], (pre * sigma).astype(BF16))
        act_sum = part if act_sum is None else act_sum + part

    acc[DEC + 0] = outer(recv[1].reshape(768, 512), dec_d[...])
    dec_sums[0].begin()
    grid_sum = dot(t_dr[...], dec_d[...]).astype(BF16)
    acc[DEC + 1] = outer(grid[...], grid_sum)
    dec_sums[1].begin()
    acc[DEC + 2] = outer(act_sum.astype(BF16), cot[...])
    dec_sums[2].begin()
    grid_out[...] = cot[...].astype(F32) + dot_back(grid_sum, w_dr[...])
    for one in dec_sums:
        one.reduce(0)

    mesh_back = None
    for o in ORDER:
        arrive(2, o)
        part = dot(t_ds[:, chunk(o)], recv[2, o])
        mesh_back = part if mesh_back is None else mesh_back + part
    gmsg = mesh_back.astype(BF16)
    high, low = split(dot_back(gmsg, w_eo[...]))
    for o in ORDER:
        back = dot(oh_er[chunk(o), :], high) + dot(oh_er[chunk(o), :], low)
        enc_d[chunk(o), :] = (back * enc_pre[chunk(o), :]).astype(BF16)
    acc[ENC + 0] = outer(recv[0].reshape(768, 512), enc_d[...])
    enc_sums[0].begin()
    mesh_sum = dot(t_er[...], enc_d[...]).astype(BF16)
    acc[ENC + 1] = outer(mesh[...], mesh_sum)
    enc_sums[1].begin()
    acc[ENC + 2] = outer(enc_act_sum, gmsg)
    enc_sums[2].begin()
    for o in ORDER:
        send[3, o] = dot_back(enc_d[chunk(o), :], w_es[...]).astype(BF16)
        edges(3, -1, o)
    mesh_out[...] = mesh_back + dot_back(mesh_sum, w_er[...])

    for one in enc_sums:
        one.reduce(0)
    for one in dec_sums:
        one.reduce(1)
    for one in enc_sums:
        one.reduce(1)
    for one in dec_sums:
        one.reduce(2)
    for one in enc_sums:
        one.reduce(2)
    total = grid_out[...]
    for o in ORDER:
        arrive(3, o)
        total = total + dot(t_es[:, chunk(o)], recv[3, o])
    grid_out[...] = total
    for s in reversed(range(STAGES)):
        for one in dec_sums + enc_sums:
            one.gather(s)

    for phase in range(4):
        for o in range(3):
            sent = send.at[phase, o] if o != 1 else send.at[phase, o, pl.ds(0, 224)]
            wait_bytes(sent, esend.at[phase, o])
    for one in sums:
        one.end()


def per_device(
    grid_latent, mesh_latent, grid_cotangent,
    enc_w_send, enc_w_recv, enc_w_out, dec_w_send, dec_w_recv, dec_w_out,
    enc_sender, enc_receiver, enc_count, dec_sender, dec_receiver, dec_count,
):
    vmem = pl.BlockSpec(memory_space=pltpu.VMEM)
    smem = pl.BlockSpec(memory_space=pltpu.SMEM)
    scratch = [
        pltpu.VMEM((4, 3, 256, 512), BF16),
        pltpu.VMEM((4, 3, 256, 512), BF16),
        pltpu.VMEM((768, 256), BF16),
        pltpu.VMEM((768, 128), BF16),
        pltpu.VMEM((768, 128), BF16),
        pltpu.VMEM((768, 256), BF16),
        pltpu.VMEM((256, 768), BF16),
        pltpu.VMEM((128, 768), BF16),
        pltpu.VMEM((128, 768), BF16),
        pltpu.VMEM((256, 768), BF16),
        pltpu.VMEM((768, 512), F32),
        pltpu.VMEM((768, 512), F32),
        pltpu.VMEM((768, 512), F32),
        pltpu.VMEM((768, 512), BF16),
        pltpu.VMEM((768, 512), BF16),
        pltpu.VMEM((6, 512, 512), F32),
        pltpu.VMEM((6, 512, 512), BF16),
    ]
    for t in range(6):
        scratch += scratch_for(PLANS[t % 3])
    scratch += [pltpu.SemaphoreType.DMA((4, 3))] * 2
    scratch += [pltpu.SemaphoreType.DMA((6, 2 * STAGES))] * 2
    square = jax.ShapeDtypeStruct((512, 512), BF16)
    results = pl.pallas_call(
        kernel,
        out_shape=[
            jax.ShapeDtypeStruct((256, 512), F32),
            jax.ShapeDtypeStruct((128, 512), F32),
        ] + [square] * 6,
        in_specs=[vmem] * 9 + [vmem, vmem, smem, vmem, vmem, smem],
        out_specs=[vmem] * 8,
        scratch_shapes=scratch,
        compiler_params=pltpu.CompilerParams(
            collective_id=0, has_side_effects=True, vmem_limit_bytes=56 << 20
        ),
    )(
        grid_latent, mesh_latent, grid_cotangent,
        enc_w_send, enc_w_recv, enc_w_out, dec_w_send, dec_w_recv, dec_w_out,
        enc_sender, enc_receiver, enc_count, dec_sender, dec_receiver, dec_count,
    )
    factor = float(NB * NP * 3 * NP * 32) ** (-0.5)
    return (results[0], results[1]) + tuple(g.astype(F32) * factor for g in results[2:])


def solution(mesh):
    in_specs = (
        P(("band", "patch"), None),
        P(("band", "patch"), None),
        P(("band", "patch"), None),
        P(),
        P(),
        P(),
        P(),
        P(),
        P(),
        P(("band", "patch"), None, None, None),
        P(("band", "patch"), None, None, None),
        P(("band", "patch"), None, None),
        P(("band", "patch"), None, None, None),
        P(("band", "patch"), None, None, None),
        P(("band", "patch"), None, None),
    )
    out_specs = (
        P(("band", "patch"), None),
        P(("band", "patch"), None),
        P(),
        P(),
        P(),
        P(),
        P(),
        P(),
    )
    return jax.shard_map(
        per_device, mesh=mesh, in_specs=in_specs, out_specs=out_specs, check_vma=False
    )
```

time: 196 us -> 94.6 us (0.48)
  other arithmetic: 48.5 us -> 6.14 us
  local copies, waits for them, and re-layouts: 31.7 us -> 3.66 us
  matrix products: 18.8 us -> 0 us
  Pallas kernels: 94.5 us -> 83.9 us
    scatter-add x5 -> x0, other arithmetic: 39.5 us -> none  [the longest x1 9.38 us: per_device(): jax.ops.segment_sum(enc_msg, enc_target, mesh_nodes)]
    dot_general x17 -> x0, matrix products: 18.8 us -> none  [the longest x6 8.51 us: product_back(): lax.dot_general(left, weight, (((1,), (1,)), ((), ())), preferred_element...]
    gather x6 -> x0, local copies, waits for them, and re-layouts: 17.4 us -> none  [the longest x1 3.32 us: per_device(): mesh_grad_new.astype(jnp.bfloat16)[enc_target]]
    pallas_call x5 -> x1, Pallas kernels: 94.5 us -> 83.9 us  [per_device(): pl.pallas_call(kernel, out_shape=[jax.ShapeDtypeStruct((256, 512), F32),...]
    another operation x6 -> x0, local copies, waits for them, and re-layouts: 5.28 us -> none  [the longest x2 1.57 us: per_device(): jax.ops.segment_sum(enc_msg, enc_target, mesh_nodes)]
    convert_element_type x4 -> x0, other arithmetic: 3.72 us -> none  [the longest x1 1.81 us: per_device(): grid_grad = grid_cotangent.astype(jnp.float32) + grid_from_decoder]
    mul x1 -> x3, other arithmetic: 2.82 us -> 6.14 us  [per_device(): g.astype(F32) * factor]
    squeeze x1 -> x0, local copies, waits for them, and re-layouts: 2.74 us -> none  [per_device(): totals[5]]
where the time goes in v2:
time: 94.6 us; the launch traced here: 94.4 us
  Pallas kernels  83.9 us (89%)
  other arithmetic  6.14 us (6%)
  local copies, waits for them, and re-layouts  3.66 us (4%)
    pallas_call x1, Pallas kernels, per_device(): pl.pallas_call(kernel, out_shape=[jax.ShapeDtypeStruct((256, 512), F32),...  83.9 us
    mul x3, other arithmetic, per_device(): g.astype(F32) * factor  6.14 us
    unnamed x18, local copies, waits for them, and re-layouts  3.66 us

profile of v2, /device:TPU:1, one launch (start us, length us, event | category | flops | bytes accessed | tf_op | source)
XLA Modules:
  0.0 94.4 jit_solution(399099253148169509)
XLA Ops:
  0.6 0.0 copy-start.6
  0.6 1.3 %copy.23.n_e = s32[1,3,8]{2,1,0:T(4,128)} copy(s32[1,3,8]{2,0,1:T(1,128)} %param.26) | data formatting | bytes 192 | tf_op args[11]
  1.9 0.0 copy-done.6
  1.9 0.6 copy.24.n_d
  2.5 83.9 %shard_map.206 = (f32[256,512]{1,0:T(8,128)}, f32[128,512]{1,0:T(8,128)}, bf16[512,512]{1,0:T(8,128)(2,1)}, bf16[512,512]{1,0:T(8,128)(2,1)}, bf16[512,512]{1,0:...) custom-call(bf16[256,512]{1,0:T(8,128)(2,1)} %grid.1, ...), custom_call_target="tpu_custom_call" | custom-call | tf_op jit(solution)/shard_map/pallas_call | solution.py:407
  86.4 0.0 copy-start.3
  86.4 0.0 copy-start.4
  86.4 2.9 %convert_multiply_fusion.4 = (f32[512,512]{1,0:T(8,128)}, f32[512,512]{1,0:T(8,128)}) fusion(bf16[512,512]{1,0:T(8,128)(2,1)} %get-tuple-element.19, bf16[512,512]{1,0:T(8,128)(2,1)} %get-tuple-element.18), kind=kLoop, calls=%fused_computation.4 | loop fusion | flops 1048576 | bytes 3145728 | tf_op jit(solution)/shard_map/mul | solution.py:425
  89.3 0.0 copy-done.3
  89.3 0.0 copy-done.4
  89.3 0.0 copy-start.1
  89.3 0.0 copy-start.2
  89.3 1.6 %convert_multiply_fusion.2 = (f32[512,512]{1,0:T(8,128)}, f32[512,512]{1,0:T(8,128)}) fusion(bf16[512,512]{1,0:T(8,128)(2,1)S(1)} %copy-done.4, bf16[512,512]{1,0:T(8,128)(2,1)S(1)} %copy-done.3), kind=kLoop, calls=%fused_computation.2 | loop fusion | flops 1048576 | bytes 3145728 | tf_op jit(solution)/shard_map/mul | solution.py:425
  90.9 0.0 copy-done.1
  90.9 0.0 copy-done.2
  90.9 0.0 copy-start
  91.0 1.6 %convert_multiply_fusion = (f32[512,512]{1,0:T(8,128)}, f32[512,512]{1,0:T(8,128)}) fusion(bf16[512,512]{1,0:T(8,128)(2,1)S(1)} %copy-done.2, bf16[512,512]{1,0:T(8,128)(2,1)S(1)} %copy-done.1), kind=kLoop, calls=%fused_computation | loop fusion | flops 1048576 | bytes 3145728 | tf_op jit(solution)/shard_map/mul | solution.py:425
  92.6 0.0 copy-done
  92.6 0.0 copy-start.5
  92.6 0.8 copy.27
  93.4 0.3 copy-done.5
  93.7 0.7 copy.28
Async XLA Ops:
  0.6 1.3 %copy-start.6 = (s32[1,3,8]{2,0,1:T(1,128)S(1)}, s32[1,3,8]{2,0,1:T(1,128)}, u32[]{:S(2)}) copy-start(s32[1,3,8]{2,0,1:T(1,128)} %param.29) | copy-start | bytes 292
  86.4 2.9 %copy-start.3 = (bf16[512,512]{1,0:T(8,128)(2,1)S(1)}, bf16[512,512]{1,0:T(8,128)(2,1)}, u32[]{:S(2)}) copy-start(bf16[512,512]{1,0:T(8,128)(2,1)} %get-tuple-element.20) | copy-start | bytes 1572868
  86.4 2.9 %copy-start.4 = (bf16[512,512]{1,0:T(8,128)(2,1)S(1)}, bf16[512,512]{1,0:T(8,128)(2,1)}, u32[]{:S(2)}) copy-start(bf16[512,512]{1,0:T(8,128)(2,1)} %get-tuple-element.21) | copy-start | bytes 1572868
  89.3 1.6 %copy-start.1 = (bf16[512,512]{1,0:T(8,128)(2,1)S(1)}, bf16[512,512]{1,0:T(8,128)(2,1)}, u32[]{:S(2)}) copy-start(bf16[512,512]{1,0:T(8,128)(2,1)} %get-tuple-element.22) | copy-start | bytes 1572868
  89.3 1.6 %copy-start.2 = (bf16[512,512]{1,0:T(8,128)(2,1)S(1)}, bf16[512,512]{1,0:T(8,128)(2,1)}, u32[]{:S(2)}) copy-start(bf16[512,512]{1,0:T(8,128)(2,1)} %get-tuple-element.23) | copy-start | bytes 1572868
  90.9 1.6 %copy-start = (f32[256,512]{1,0:T(8,128)S(1)}, f32[256,512]{1,0:T(8,128)}, u32[]{:S(2)}) copy-start(f32[256,512]{1,0:T(8,128)} %get-tuple-element.38) | copy-start | bytes 1572868
  92.6 1.1 %copy-start.5 = (f32[128,512]{1,0:T(8,128)S(1)}, f32[128,512]{1,0:T(8,128)}, u32[]{:S(2)}) copy-start(f32[128,512]{1,0:T(8,128)} %get-tuple-element.39) | copy-start | bytes 786436

commit v3 on v2

v3 whole, which is shorter than its diff:
```python
import functools
import itertools

import jax
import jax.numpy as jnp
from jax import lax
from jax.experimental import pallas as pl
from jax.experimental.pallas import tpu as pltpu
from jax.sharding import PartitionSpec as P


MESH = pl.DeviceIdType.MESH
NB, NP = 16, 8
SIZES = {"z": 4, "x": 4, "y": 4, "c": 2}

def position():
    b, p = lax.axis_index("band"), lax.axis_index("patch")
    return {"z": b // 4, "x": lax.rem(b, 4), "y": p // 2, "c": lax.rem(p, 2)}

def device(pos):
    return (pos["z"] * 4 + pos["x"], pos["y"] * 2 + pos["c"])

def offsets(axes):
    return [d for d in itertools.product(*[range(SIZES[a]) for a in axes]) if any(d)]

def partner(pos, axes, d):
    new = dict(pos)
    for a, k in zip(axes, d):
        new[a] = lax.rem(pos[a] + k, SIZES[a])
    return new

def index(pos, axes):
    i = 0
    for a in axes:
        i = i * SIZES[a] + pos[a]
    return i

def geometry(plan):
    R = C = 512
    out = []
    for axes in plan:
        g = 1
        for a in axes:
            g *= SIZES[a]
        rs = min(g, R // 16)
        cs = g // rs
        out.append((axes, g, (R, C), (R // rs, C // cs), cs))
        R, C = R // rs, C // cs
    return out

def scratch_for(plan):
    shapes = []
    for axes, g, (R, C), (pr, pc), cs in geometry(plan):
        shapes += [pltpu.VMEM((pr, pc), jnp.float32), pltpu.VMEM((pr, pc), jnp.bfloat16), pltpu.VMEM((g - 1, pr, pc), jnp.bfloat16)]
    return shapes

def piece(k, cs, pr, pc):
    r = (k // cs) * pr
    c = lax.rem(k, cs) * pc if cs > 1 else 0
    r = pl.multiple_of(r, 16) if not isinstance(r, int) else r
    if cs > 1: c = pl.multiple_of(c, 128)
    return r, c

def rs_send(pos, geo, s, srcb, recv, ssem, rsem):
    axes, g, _, (pr, pc), cs = geo[s]
    for n, d in enumerate(offsets(axes)):
        to = partner(pos, axes, d)
        r, c = piece(index(to, axes), cs, pr, pc)
        pltpu.make_async_remote_copy(srcb.at[pl.ds(r, pr), pl.ds(c, pc)], recv.at[n], ssem, rsem, device_id=device(to), device_id_type=MESH).start()

def wait_bytes(ref, sem):
    pltpu.make_async_copy(ref, ref, sem).wait()

def rs_sum(pos, geo, s, cur, recv, rsem):
    axes, g, _, (pr, pc), cs = geo[s]
    wait_bytes(recv, rsem)
    r, c = piece(index(pos, axes), cs, pr, pc)
    total = cur[pl.ds(r, pr), pl.ds(c, pc)]
    for n in range(g - 1):
        total = total + recv[n].astype(jnp.float32)
    return total

def regions(pos, geo):
    r0 = c0 = 0
    out = [(0, 0)]
    for axes, g, _, (pr, pc), cs in geo:
        r, c = piece(index(pos, axes), cs, pr, pc)
        r0, c0 = r0 + r, c0 + c
        out.append((pl.multiple_of(r0, 16), pl.multiple_of(c0, 128)))
    return out

def ag_send(pos, geo, regs, s, out, ssem, rsem):
    axes, g, _, (pr, pc), cs = geo[s]
    r, c = regs[s + 1]
    view = out.at[pl.ds(r, pr), pl.ds(c, pc)]
    for n, d in enumerate(offsets(axes)):
        to = partner(pos, axes, d)
        pltpu.make_async_remote_copy(view, view, ssem, rsem, device_id=device(to), device_id_type=MESH).start()


F32, BF16 = jnp.float32, jnp.bfloat16
OUT_ORDER = (2, 1, 3, 0)
IN_ORDER = (2, 1, 3, 0)
TAIL = (
    "s", "e0", "m", "d1", "e1", "d2", "e2", "d3", "R2", "e3", "R1", "R3", "R0",
    "e4", "d4", "e5", "d5", "g",
)
BLOCKS = [(o, dc) for o in range(3) for dc in range(2)]
ROWS = 32 * len(BLOCKS)
PLANS = [
    ("c", "z", "xy"), ("c", "x", "zy"), ("c", "z", "xy"),
    ("c", "y", "xz"), ("c", "x", "zy"), ("c", "z", "xy"),
]
GEO = [geometry(plan) for plan in PLANS]
FACTOR = float(NB * NP * 3 * NP * 32) ** (-0.5)
STAGES = 3
DEC, ENC = 0, 3


def dot(left, right):
    return jnp.dot(left, right, preferred_element_type=F32)


def dot_back(left, weight):
    return lax.dot_general(left, weight, (((1,), (1,)), ((), ())), preferred_element_type=F32)


def outer(left, right):
    return lax.dot_general(left, right, (((0,), (0,)), ((), ())), preferred_element_type=F32)


def split(value):
    high = value.astype(BF16)
    return high, (value - high.astype(F32)).astype(BF16)


def sigmoid(value):
    return 1.0 / (1.0 + jnp.exp(-value))


def chunk(dy):
    return pl.ds(dy * ROWS, ROWS)


def patch_at(pos, sign, dy, dc):
    return lax.rem(pos["y"] + sign * dy + 4, 4) * 2 + lax.rem(pos["c"] + dc, 2)


def live_only(ref, count, o):
    columns = jnp.transpose(ref[0, o])
    slot = lax.broadcasted_iota(jnp.int32, (32, NP), 0)
    return jnp.transpose(jnp.where(slot < count[o], columns, -1))


def pick(row_of, pos, sign, dy, rows):
    lines = [row_of(o, patch_at(pos, sign, dy, dc)) for o, dc in BLOCKS]
    columns = jnp.transpose(jnp.concatenate(lines + lines[:2], axis=0))
    node = lax.broadcasted_iota(jnp.int32, (32, rows), 1)
    parts = []
    for n in range(len(BLOCKS)):
        parts.append(jnp.where(node == columns[:, n : n + 1], 1.0, 0.0).astype(BF16))
    return jnp.concatenate(parts, axis=0)


def edge_send(sign, dy, b, pos, send, recv, send_sem, recv_sem):
    for n, (o, dc) in enumerate(BLOCKS):
        band = lax.rem(b + sign * (o - 1) + NB, NB)
        src = send.at[dy, pl.ds(n * 32, 32)]
        dst = recv.at[dy, pl.ds(n * 32, 32)]
        if (o, dy, dc) == (1, 0, 0):
            pltpu.make_async_copy(src, dst, recv_sem.at[dy]).start()
        else:
            pltpu.make_async_remote_copy(
                src, dst, send_sem.at[dy], recv_sem.at[dy],
                device_id=(band, patch_at(pos, sign, dy, dc)), device_id_type=MESH,
            ).start()


def greet(b, p, pos):
    bar = pltpu.get_barrier_semaphore()
    n = 0
    for dy in OUT_ORDER:
        for o, dc in BLOCKS:
            if (o, dy, dc) != (1, 0, 0):
                band = lax.rem(b + o - 1 + NB, NB)
                pl.semaphore_signal(
                    bar, inc=1, device_id=(band, patch_at(pos, 1, dy, dc)), device_id_type=MESH
                )
                n += 1
    seen = []
    for plan in PLANS:
        for axes in plan:
            for d in offsets(axes):
                full = tuple(dict(zip(axes, d)).get(a, 0) for a in "zxyc")
                if full not in seen:
                    seen.append(full)
    for d in seen:
        pl.semaphore_signal(
            bar, inc=1, device_id=device(partner(pos, "zxyc", d)), device_id_type=MESH
        )
    return bar, n + len(seen)


class Sum:
    def __init__(self, pos, t, acc, sbf, scr, out, ssem, rsem):
        self.pos, self.geo = pos, GEO[t]
        self.acc, self.sbf, self.out = acc.at[t], sbf.at[t], out.at[t]
        self.scr, self.t = scr[t], t
        self.ssem, self.rsem = ssem, rsem
        self.sibling = partner(pos, "c", (1,))
        self.axis = PLANS[t][1]
        self.half = pos["c"] * 256

    def begin(self):
        other = pl.ds(pl.multiple_of((1 - self.pos["c"]) * 256, 256), 256)
        self.sbf[other, :] = self.acc[other, :].astype(BF16)
        rs_send(self.pos, self.geo, 0, self.sbf, self.scr[0][2],
                self.ssem.at[self.t, 0], self.rsem.at[self.t, 0])

    def reduce(self, s):
        pos, geo, scr, t = self.pos, self.geo, self.scr, self.t
        cur = self.acc if s == 0 else scr[s - 1][0]
        total = rs_sum(pos, geo, s, cur, scr[s][2], self.rsem.at[t, s])
        if s < 2:
            scr[s][0][...] = total
            scr[s][1][...] = total.astype(BF16)
            rs_send(pos, geo, s + 1, scr[s][1], scr[s + 1][2],
                    self.ssem.at[t, s + 1], self.rsem.at[t, s + 1])
        else:
            pr, pc = geo[s][3]
            regs = regions(pos, geo)
            r, c = regs[-1]
            self.out[pl.ds(r, pr), pl.ds(c, pc)] = total.astype(BF16)
            ag_send(pos, geo, regs, 2, self.out, self.ssem.at[t, 4], self.rsem.at[t, 4])

    def rows(self, k):
        place = lax.rem(self.pos[self.axis] - k + 4, 4)
        return self.out.at[pl.ds(pl.multiple_of(self.half + place * 64, 64), 64), :]

    def pass_on(self, k):
        view = self.rows(k)
        pltpu.make_async_remote_copy(
            view, view, self.ssem.at[self.t, 3], self.rsem.at[self.t, 3],
            device_id=device(self.sibling), device_id_type=MESH,
        ).start()

    def gather_plane(self):
        t = self.t
        wait_bytes(self.scr[2][2], self.rsem.at[t, 4])
        view = self.rows(0)
        for d in (2, 1, 3):
            to = partner(self.pos, self.axis, (d,))
            pltpu.make_async_remote_copy(
                view, view, self.ssem.at[t, 5], self.rsem.at[t, 4 + d],
                device_id=device(to), device_id_type=MESH,
            ).start()
        self.pass_on(0)

    def gather_axis(self, d):
        wait_bytes(self.rows(d), self.rsem.at[self.t, 4 + d])
        self.pass_on(d)

    def gather_pair(self):
        wait_bytes(self.scr[0][2], self.rsem.at[self.t, 3])

    def end(self):
        t, scr = self.t, self.scr
        for place, ref in enumerate((scr[0], scr[1], scr[2], scr[0], scr[2], scr[1])):
            wait_bytes(ref[2], self.ssem.at[t, place])


def kernel(
    grid, mesh_in, cot_in, es_in, er_in, eo_in, ds_in, dr_in, do_in,
    i_es, i_er, n_e, i_ds, i_dr, n_d,
    grid_res, mesh_res, o0, o1, o2, o3, o4, o5,
    mesh, cot, w_es, w_er, w_eo, w_ds, w_dr, w_do, grid_out, mesh_out, out,
    isem, osem, live, send, recv, oh_es, oh_er, oh_ds, oh_dr, t_es, t_er, t_ds, t_dr,
    enc_pre, dec_pre, dec_back, enc_d, dec_d, acc, sbf, *rest,
):
    scr = []
    for t in range(6):
        n = 9 * t
        scr.append([rest[n + 3 * s : n + 3 * s + 3] for s in range(STAGES)])
    esend, erecv, ssem, rsem = rest[54:]
    results = [o3, o4, o5, o0, o1, o2]
    loads = {}
    for n, (name, src, dst) in enumerate((
        ("er", er_in, w_er), ("mesh", mesh_in, mesh), ("dr", dr_in, w_dr), ("cot", cot_in, cot),
        ("do", do_in, w_do), ("es", es_in, w_es), ("eo", eo_in, w_eo), ("ds", ds_in, w_ds),
    )):
        loads[name] = pltpu.make_async_copy(src, dst, isem.at[n])
        loads[name].start()

    def store(n, src, dst):
        copy = pltpu.make_async_copy(src, dst, osem.at[n])
        copy.start()
        return copy

    b, p = lax.axis_index("band"), lax.axis_index("patch")
    pos = position()
    bar, greeted = greet(b, p, pos)

    def edges(phase, sign, dy):
        edge_send(sign, dy, b, pos, send.at[phase], recv.at[phase], esend.at[phase], erecv.at[phase])

    def arrive(phase, o):
        wait_bytes(recv.at[phase, o], erecv.at[phase, o])

    sums = [Sum(pos, t, acc, sbf, scr, out, ssem, rsem) for t in range(6)]
    dec_sums, enc_sums = sums[:3], sums[3:]

    for n, dy in enumerate(OUT_ORDER):
        oh_es[chunk(dy), :] = pick(lambda o, q: i_es[0, o, pl.ds(q, 1), :], pos, 1, dy, 256)
        send[0, dy] = dot(oh_es[chunk(dy), :], grid[...]).astype(BF16)
        if n == 0:
            pl.semaphore_wait(bar, greeted)
        edges(0, 1, dy)

    for o in range(3):
        live[0, o] = live_only(i_er, n_e, o)
        live[1, o] = live_only(i_dr, n_d, o)
    for dy in range(4):
        oh_er[chunk(dy), :] = pick(lambda o, q: live[0, o, pl.ds(q, 1), :], pos, -1, dy, 128)
    t_er[...] = jnp.transpose(oh_er[...])
    loads["er"].wait()
    loads["mesh"].wait()
    high, low = split(dot(mesh[...], w_er[...]))
    for dy in range(4):
        enc_pre[chunk(dy), :] = dot(oh_er[chunk(dy), :], high) + dot(oh_er[chunk(dy), :], low)
    for dy in range(4):
        oh_ds[chunk(dy), :] = pick(lambda o, q: i_ds[0, o, pl.ds(q, 1), :], pos, 1, dy, 128)
        oh_dr[chunk(dy), :] = pick(lambda o, q: live[1, o, pl.ds(q, 1), :], pos, -1, dy, 256)
    t_ds[...] = jnp.transpose(oh_ds[...])
    t_dr[...] = jnp.transpose(oh_dr[...])
    t_es[...] = jnp.transpose(oh_es[...])
    loads["dr"].wait()
    high, low = split(dot(grid[...], w_dr[...]))
    for dy in range(4):
        dec_pre[chunk(dy), :] = dot(oh_dr[chunk(dy), :], high) + dot(oh_dr[chunk(dy), :], low)
    loads["cot"].wait()
    loads["do"].wait()
    high, low = split(dot_back(cot[...], w_do[...]))
    for dy in range(4):
        dec_back[chunk(dy), :] = dot(oh_dr[chunk(dy), :], high) + dot(oh_dr[chunk(dy), :], low)

    for name in ("es", "eo", "ds"):
        loads[name].wait()
    for dy in IN_ORDER:
        arrive(0, dy)
        pre = dot(recv[0, dy], w_es[...]) + enc_pre[chunk(dy), :]
        enc_pre[chunk(dy), :] = pre
        enc_d[chunk(dy), :] = (pre * sigmoid(pre)).astype(BF16)
    high, low = split(dot(t_er[...], enc_d[...]))
    mesh_new = (mesh[...].astype(F32) + (dot(high, w_eo[...]) + dot(low, w_eo[...]))).astype(BF16)
    enc_act_sum = high

    for dy in OUT_ORDER:
        send[1, dy] = dot(oh_ds[chunk(dy), :], mesh_new).astype(BF16)
        edges(1, 1, dy)
    for dy in range(4):
        pre = enc_pre[chunk(dy), :]
        sigma = sigmoid(pre)
        enc_pre[chunk(dy), :] = sigma * (1.0 + pre * (1.0 - sigma))

    for dy in IN_ORDER:
        arrive(1, dy)
        pre = dot(recv[1, dy], w_ds[...]) + dec_pre[chunk(dy), :]
        sigma = sigmoid(pre)
        slope = sigma * (1.0 + pre * (1.0 - sigma))
        dpre = (dec_back[chunk(dy), :] * slope).astype(BF16)
        dec_d[chunk(dy), :] = dpre
        send[2, dy] = dot_back(dpre, w_ds[...]).astype(BF16)
        edges(2, -1, dy)
        enc_d[chunk(dy), :] = (pre * sigma).astype(BF16)

    acc[DEC + 0] = outer(recv[1].reshape(768, 512), dec_d[...])
    dec_sums[0].begin()
    grid_sum = dot(t_dr[...], dec_d[...]).astype(BF16)
    acc[DEC + 1] = outer(grid[...], grid_sum)
    dec_sums[1].begin()
    acc[DEC + 2] = outer(dot(t_dr[...], enc_d[...]).astype(BF16), cot[...])
    dec_sums[2].begin()
    grid_out[...] = cot[...].astype(F32) + dot_back(grid_sum, w_dr[...])
    for one in dec_sums:
        one.reduce(0)
    for dy in IN_ORDER:
        arrive(2, dy)
    mesh_back = dot(t_ds[...], recv[2].reshape(768, 512))
    gmsg = mesh_back.astype(BF16)
    acc[ENC + 2] = outer(enc_act_sum, gmsg)
    enc_sums[2].begin()
    high, low = split(dot_back(gmsg, w_eo[...]))
    for dy in range(4):
        back = dot(oh_er[chunk(dy), :], high) + dot(oh_er[chunk(dy), :], low)
        enc_d[chunk(dy), :] = (back * enc_pre[chunk(dy), :]).astype(BF16)
    acc[ENC + 0] = outer(recv[0].reshape(768, 512), enc_d[...])
    enc_sums[0].begin()
    mesh_sum = dot(t_er[...], enc_d[...]).astype(BF16)
    acc[ENC + 1] = outer(mesh[...], mesh_sum)
    enc_sums[1].begin()

    stores = []

    def advance(group, n):
        if n == 4:
            for d in (1, 3, 2):
                for one in group:
                    one.gather_axis(d)
            return
        for one in group:
            if n < 3:
                one.reduce(n)
            elif n == 3:
                one.gather_plane()
            else:
                one.gather_pair()
                stores.append(store(one.t, one.out, results[one.t]))

    for token in TAIL:
        if token[0] == "d":
            advance(dec_sums, int(token[1]))
        elif token[0] == "e":
            advance((enc_sums[2], enc_sums[0], enc_sums[1]), int(token[1]))
        elif token[0] == "R":
            edges(3, -1, int(token[1]))
        elif token == "s":
            for dy in OUT_ORDER:
                send[3, dy] = dot_back(enc_d[chunk(dy), :], w_es[...]).astype(BF16)
        elif token == "m":
            mesh_out[...] = mesh_back + dot_back(mesh_sum, w_er[...])
            stores.append(store(6, mesh_out, mesh_res))
        elif token == "g":
            for dy in OUT_ORDER:
                arrive(3, dy)
            grid_out[...] = grid_out[...] + dot(t_es[...], recv[3].reshape(768, 512))
            stores.append(store(7, grid_out, grid_res))

    for phase in range(4):
        for dy in range(4):
            sent = send.at[phase, dy] if dy else send.at[phase, dy, pl.ds(0, ROWS - 32)]
            wait_bytes(sent, esend.at[phase, dy])
    for one in sums:
        one.end()
    for one in stores:
        one.wait()


def finish(grid_in, mesh_in, *refs):
    sums, (grid_out, mesh_out), outs = refs[:6], refs[6:8], refs[8:14]
    narrow, wide, grid_rows, mesh_rows, in_sem, out_sem = refs[14:]
    loads = [pltpu.make_async_copy(sums[t], narrow.at[t], in_sem.at[t]) for t in range(6)]
    stores = [pltpu.make_async_copy(wide.at[t], outs[t], out_sem.at[t]) for t in range(6)]
    loads.append(pltpu.make_async_copy(grid_in, grid_rows, in_sem.at[6]))
    loads.append(pltpu.make_async_copy(mesh_in, mesh_rows, in_sem.at[7]))
    stores.append(pltpu.make_async_copy(grid_rows, grid_out, out_sem.at[6]))
    stores.append(pltpu.make_async_copy(mesh_rows, mesh_out, out_sem.at[7]))
    for n in (6, 0, 1, 2, 3, 4, 5, 7):
        loads[n].start()
    for n in (6, 7):
        loads[n].wait()
        stores[n].start()
    for t in range(6):
        loads[t].wait()
        wide[t] = narrow[t].astype(F32) * FACTOR
        stores[t].start()
    for one in stores:
        one.wait()


def per_device(
    grid_latent, mesh_latent, grid_cotangent,
    enc_w_send, enc_w_recv, enc_w_out, dec_w_send, dec_w_recv, dec_w_out,
    enc_sender, enc_receiver, enc_count, dec_sender, dec_receiver, dec_count,
):
    vmem = pl.BlockSpec(memory_space=pltpu.VMEM)
    anywhere = pl.BlockSpec(memory_space=pl.ANY)
    weight = pltpu.VMEM((512, 512), BF16)
    scratch = [
        pltpu.VMEM((128, 512), BF16),
        pltpu.VMEM((256, 512), BF16),
    ] + [weight] * 6 + [
        pltpu.VMEM((256, 512), F32),
        pltpu.VMEM((128, 512), F32),
        pltpu.VMEM((6, 512, 512), BF16),
        pltpu.SemaphoreType.DMA((8,)),
        pltpu.SemaphoreType.DMA((8,)),
        pltpu.VMEM((2, 3, NP, 32), jnp.int32),
        pltpu.VMEM((4, 4, ROWS, 512), BF16),
        pltpu.VMEM((4, 4, ROWS, 512), BF16),
        pltpu.VMEM((768, 256), BF16),
        pltpu.VMEM((768, 128), BF16),
        pltpu.VMEM((768, 128), BF16),
        pltpu.VMEM((768, 256), BF16),
        pltpu.VMEM((256, 768), BF16),
        pltpu.VMEM((128, 768), BF16),
        pltpu.VMEM((128, 768), BF16),
        pltpu.VMEM((256, 768), BF16),
        pltpu.VMEM((768, 512), F32),
        pltpu.VMEM((768, 512), F32),
        pltpu.VMEM((768, 512), F32),
        pltpu.VMEM((768, 512), BF16),
        pltpu.VMEM((768, 512), BF16),
        pltpu.VMEM((6, 512, 512), F32),
        pltpu.VMEM((6, 512, 512), BF16),
    ]
    for t in range(6):
        scratch += scratch_for(PLANS[t])
    scratch += [pltpu.SemaphoreType.DMA((4, 4))] * 2
    scratch += [pltpu.SemaphoreType.DMA((6, 6)), pltpu.SemaphoreType.DMA((6, 8))]
    square = jax.ShapeDtypeStruct((512, 512), BF16)
    rows = [jax.ShapeDtypeStruct((256, 512), F32), jax.ShapeDtypeStruct((128, 512), F32)]
    results = pl.pallas_call(
        kernel,
        out_shape=rows + [square] * 6,
        in_specs=[vmem] + [anywhere] * 8 + [vmem] * 6,
        out_specs=[anywhere] * 8,
        scratch_shapes=scratch,
        compiler_params=pltpu.CompilerParams(
            collective_id=0, has_side_effects=True, vmem_limit_bytes=56 << 20
        ),
    )(
        grid_latent, mesh_latent, grid_cotangent,
        enc_w_send, enc_w_recv, enc_w_out, dec_w_send, dec_w_recv, dec_w_out,
        enc_sender, enc_receiver, jnp.transpose(enc_count, (1, 0, 2)),
        dec_sender, dec_receiver, jnp.transpose(dec_count, (1, 0, 2)),
    )
    return pl.pallas_call(
        finish,
        out_shape=rows + [jax.ShapeDtypeStruct((512, 512), F32)] * 6,
        in_specs=[anywhere] * 8,
        out_specs=[anywhere] * 8,
        scratch_shapes=[
            pltpu.VMEM((6, 512, 512), BF16),
            pltpu.VMEM((6, 512, 512), F32),
            pltpu.VMEM((256, 512), F32),
            pltpu.VMEM((128, 512), F32),
            pltpu.SemaphoreType.DMA((8,)),
            pltpu.SemaphoreType.DMA((8,)),
        ],
        compiler_params=pltpu.CompilerParams(vmem_limit_bytes=60 << 20),
    )(*results)


def solution(mesh):
    in_specs = (
        P(("band", "patch"), None),
        P(("band", "patch"), None),
        P(("band", "patch"), None),
        P(),
        P(),
        P(),
        P(),
        P(),
        P(),
        P(("band", "patch"), None, None, None),
        P(("band", "patch"), None, None, None),
        P(("band", "patch"), None, None),
        P(("band", "patch"), None, None, None),
        P(("band", "patch"), None, None, None),
        P(("band", "patch"), None, None),
    )
    out_specs = (
        P(("band", "patch"), None),
        P(("band", "patch"), None),
        P(),
        P(),
        P(),
        P(),
        P(),
        P(),
    )
    return jax.shard_map(
        per_device, mesh=mesh, in_specs=in_specs, out_specs=out_specs, check_vma=False
    )
```

time: 94.6 us -> 89.3 us (0.944)
  other arithmetic: 6.14 us -> 0 us
  Pallas kernels: 83.9 us -> 88.5 us
  local copies, waits for them, and re-layouts: 3.66 us -> 0 us
    mul x3 -> x0, other arithmetic: 6.14 us -> none  [per_device(): g.astype(F32) * factor]
    pallas_call x1 -> x2, Pallas kernels: 83.9 us -> 88.5 us  [the longest x1 83.4 us: per_device(): pl.pallas_call(kernel, out_shape=rows + [square] * 6, in_specs=[vmem] + [...]
    unnamed x18 -> x0, local copies, waits for them, and re-layouts: 3.66 us -> none
where the time goes in v3:
time: 89.3 us; the launch traced here: 89.2 us
  Pallas kernels  88.5 us (99%)
    pallas_call x1, Pallas kernels, per_device(): pl.pallas_call(kernel, out_shape=rows + [square] * 6, in_specs=[vmem] + [...  83.4 us
    pallas_call x1, Pallas kernels, per_device(): pl.pallas_call(finish, out_shape=rows + [jax.ShapeDtypeStruct((512, 512),...  5.14 us

profile of v3, /device:TPU:1, one launch (start us, length us, event | category | flops | bytes accessed | tf_op | source)
XLA Modules:
  0.0 89.2 jit_solution(2147577228288875785)
XLA Ops:
  0.6 83.4 %shard_map.206 = (f32[256,512]{1,0:T(8,128)}, f32[128,512]{1,0:T(8,128)}, bf16[512,512]{1,0:T(8,128)(2,1)}, bf16[512,512]{1,0:T(8,128)(2,1)}, bf16[512,512]{1,0:...) custom-call(bf16[256,512]{1,0:T(8,128)(2,1)} %grid.1, ...), custom_call_target="tpu_custom_call" | custom-call | tf_op jit(solution)/shard_map/pallas_call | solution.py:512
  84.0 5.1 %shard_map.207 = (f32[256,512]{1,0:T(8,128)}, f32[128,512]{1,0:T(8,128)}, f32[512,512]{1,0:T(8,128)}, f32[512,512]{1,0:T(8,128)}, f32[512,512]{1,0:T(8,128)}, /*...) custom-call(f32[256,512]{1,0:T(8,128)} %get-tuple-element.16.grid_in, ...), custom_call_target="tpu_custom_call" | custom-call | tf_op jit(solution)/shard_map/pallas_call | solution.py:527

commit v4 on v3

--- a/solution.py
+++ b/solution.py
@@ -102,7 +102,7 @@
 OUT_ORDER = (2, 1, 3, 0)
 IN_ORDER = (2, 1, 3, 0)
 TAIL = (
-    "s", "e0", "m", "d1", "e1", "d2", "e2", "d3", "R2", "e3", "R1", "R3", "R0",
+    "s", "e0", "m", "d1", "e1", "d2", "e2", "A0", "A1", "d3", "e3", "B0", "B1", "R0",
     "e4", "d4", "e5", "d5", "g",
 )
 BLOCKS = [(o, dc) for o in range(3) for dc in range(2)]
@@ -162,8 +162,10 @@
     return jnp.concatenate(parts, axis=0)
 
 
-def edge_send(sign, dy, b, pos, send, recv, send_sem, recv_sem):
+def edge_send(sign, dy, b, pos, send, recv, send_sem, recv_sem, cores=(0, 1)):
     for n, (o, dc) in enumerate(BLOCKS):
+        if dc not in cores:
+            continue
         band = lax.rem(b + sign * (o - 1) + NB, NB)
         src = send.at[dy, pl.ds(n * 32, 32)]
         dst = recv.at[dy, pl.ds(n * 32, 32)]
@@ -270,10 +272,10 @@
 
 
 def kernel(
-    grid, mesh_in, cot_in, es_in, er_in, eo_in, ds_in, dr_in, do_in,
-    i_es, i_er, n_e, i_ds, i_dr, n_d,
+    grid_in, mesh_in, cot_in, es_in, er_in, eo_in, ds_in, dr_in, do_in,
+    es_i, er_i, n_e_in, ds_i, dr_i, n_d_in,
     grid_res, mesh_res, o0, o1, o2, o3, o4, o5,
-    mesh, cot, w_es, w_er, w_eo, w_ds, w_dr, w_do, grid_out, mesh_out, out,
+    grid, i_es, i_er, n_e, i_ds, i_dr, n_d, mesh, cot, w_es, w_er, w_eo, w_ds, w_dr, w_do, grid_out, mesh_out, out,
     isem, osem, live, send, recv, oh_es, oh_er, oh_ds, oh_dr, t_es, t_er, t_ds, t_dr,
     enc_pre, dec_pre, dec_back, enc_d, dec_d, acc, sbf, *rest,
 ):
@@ -285,7 +287,8 @@
     results = [o3, o4, o5, o0, o1, o2]
     loads = {}
     for n, (name, src, dst) in enumerate((
-        ("er", er_in, w_er), ("mesh", mesh_in, mesh), ("dr", dr_in, w_dr), ("cot", cot_in, cot),
+        ("i_es", es_i, i_es), ("grid", grid_in, grid), ("i_er", er_i, i_er), ("n_e", n_e_in, n_e),
+        ("i_ds", ds_i, i_ds), ("i_dr", dr_i, i_dr), ("n_d", n_d_in, n_d), ("er", er_in, w_er), ("mesh", mesh_in, mesh), ("dr", dr_in, w_dr), ("cot", cot_in, cot),
         ("do", do_in, w_do), ("es", es_in, w_es), ("eo", eo_in, w_eo), ("ds", ds_in, w_ds),
     )):
         loads[name] = pltpu.make_async_copy(src, dst, isem.at[n])
@@ -300,8 +303,9 @@
     pos = position()
     bar, greeted = greet(b, p, pos)
 
-    def edges(phase, sign, dy):
-        edge_send(sign, dy, b, pos, send.at[phase], recv.at[phase], esend.at[phase], erecv.at[phase])
+    def edges(phase, sign, dy, cores=(0, 1)):
+        edge_send(sign, dy, b, pos, send.at[phase], recv.at[phase],
+                  esend.at[phase], erecv.at[phase], cores)
 
     def arrive(phase, o):
         wait_bytes(recv.at[phase, o], erecv.at[phase, o])
@@ -309,6 +313,8 @@
     sums = [Sum(pos, t, acc, sbf, scr, out, ssem, rsem) for t in range(6)]
     dec_sums, enc_sums = sums[:3], sums[3:]
 
+    loads["i_es"].wait()
+    loads["grid"].wait()
     for n, dy in enumerate(OUT_ORDER):
         oh_es[chunk(dy), :] = pick(lambda o, q: i_es[0, o, pl.ds(q, 1), :], pos, 1, dy, 256)
         send[0, dy] = dot(oh_es[chunk(dy), :], grid[...]).astype(BF16)
@@ -316,6 +322,8 @@
             pl.semaphore_wait(bar, greeted)
         edges(0, 1, dy)
 
+    for name in ("i_er", "n_e", "i_ds", "i_dr", "n_d"):
+        loads[name].wait()
     for o in range(3):
         live[0, o] = live_only(i_er, n_e, o)
         live[1, o] = live_only(i_dr, n_d, o)
@@ -421,8 +429,9 @@
             advance(dec_sums, int(token[1]))
         elif token[0] == "e":
             advance((enc_sums[2], enc_sums[0], enc_sums[1]), int(token[1]))
-        elif token[0] == "R":
-            edges(3, -1, int(token[1]))
+        elif token[0] in "RAB":
+            for dy in {"R": (0,), "A": (2,), "B": (1, 3)}[token[0]]:
+                edges(3, -1, dy, (0, 1) if token[0] == "R" else (int(token[1]),))
         elif token == "s":
             for dy in OUT_ORDER:
                 send[3, dy] = dot_back(enc_d[chunk(dy), :], w_es[...]).astype(BF16)
@@ -472,17 +481,20 @@
     enc_w_send, enc_w_recv, enc_w_out, dec_w_send, dec_w_recv, dec_w_out,
     enc_sender, enc_receiver, enc_count, dec_sender, dec_receiver, dec_count,
 ):
-    vmem = pl.BlockSpec(memory_space=pltpu.VMEM)
     anywhere = pl.BlockSpec(memory_space=pl.ANY)
     weight = pltpu.VMEM((512, 512), BF16)
+    index = pltpu.VMEM((1, 3, NP, 32), jnp.int32)
+    count = pltpu.VMEM((3, 1, NP), jnp.int32)
     scratch = [
+        pltpu.VMEM((256, 512), BF16),
+        index, index, count, index, index, count,
         pltpu.VMEM((128, 512), BF16),
         pltpu.VMEM((256, 512), BF16),
     ] + [weight] * 6 + [
         pltpu.VMEM((256, 512), F32),
         pltpu.VMEM((128, 512), F32),
         pltpu.VMEM((6, 512, 512), BF16),
-        pltpu.SemaphoreType.DMA((8,)),
+        pltpu.SemaphoreType.DMA((15,)),
         pltpu.SemaphoreType.DMA((8,)),
         pltpu.VMEM((2, 3, NP, 32), jnp.int32),
         pltpu.VMEM((4, 4, ROWS, 512), BF16),
@@ -512,7 +524,7 @@
     results = pl.pallas_call(
         kernel,
         out_shape=rows + [square] * 6,
-        in_specs=[vmem] + [anywhere] * 8 + [vmem] * 6,
+        in_specs=[anywhere] * 15,
         out_specs=[anywhere] * 8,
         scratch_shapes=scratch,
         compiler_params=pltpu.CompilerParams(

time: 89.3 us -> 88.5 us (level)
  no operation moved by 1% of the time
where the time goes in v4:
time: 88.5 us; the launch traced here: 88.3 us
  Pallas kernels  87.7 us (99%)
    pallas_call x1, Pallas kernels, per_device(): pl.pallas_call(kernel, out_shape=rows + [square] * 6, in_specs=[anywhere]...  82.6 us
    pallas_call x1, Pallas kernels, per_device(): pl.pallas_call(finish, out_shape=rows + [jax.ShapeDtypeStruct((512, 512),...  5.14 us

profile of v4, /device:TPU:1, one launch (start us, length us, event | category | flops | bytes accessed | tf_op | source)
XLA Modules:
  0.0 88.3 jit_solution(14123867326940962139)
XLA Ops:
  0.6 82.6 %shard_map.206 = (f32[256,512]{1,0:T(8,128)}, f32[128,512]{1,0:T(8,128)}, bf16[512,512]{1,0:T(8,128)(2,1)}, bf16[512,512]{1,0:T(8,128)(2,1)}, bf16[512,512]{1,0:...) custom-call(bf16[256,512]{1,0:T(8,128)(2,1)} %grid_in.1, ...), custom_call_target="tpu_custom_call" | custom-call | tf_op jit(solution)/shard_map/pallas_call | solution.py:524
  83.2 5.1 %shard_map.207 = (f32[256,512]{1,0:T(8,128)}, f32[128,512]{1,0:T(8,128)}, f32[512,512]{1,0:T(8,128)}, f32[512,512]{1,0:T(8,128)}, f32[512,512]{1,0:T(8,128)}, /*...) custom-call(f32[256,512]{1,0:T(8,128)} %get-tuple-element.16.grid_in, ...), custom_call_target="tpu_custom_call" | custom-call | tf_op jit(solution)/shard_map/pallas_call | solution.py:539

commit v5 on v4

--- a/solution.py
+++ b/solution.py
@@ -276,7 +276,7 @@
     es_i, er_i, n_e_in, ds_i, dr_i, n_d_in,
     grid_res, mesh_res, o0, o1, o2, o3, o4, o5,
     grid, i_es, i_er, n_e, i_ds, i_dr, n_d, mesh, cot, w_es, w_er, w_eo, w_ds, w_dr, w_do, grid_out, mesh_out, out,
-    isem, osem, live, send, recv, oh_es, oh_er, oh_ds, oh_dr, t_es, t_er, t_ds, t_dr,
+    isem, osem, live, t_rows, t_mesh, t_act, send, recv, oh_es, oh_er, oh_ds, oh_dr, t_es, t_er, t_ds, t_dr,
     enc_pre, dec_pre, dec_back, enc_d, dec_d, acc, sbf, *rest,
 ):
     scr = []
@@ -370,6 +370,10 @@
         sigma = sigmoid(pre)
         enc_pre[chunk(dy), :] = sigma * (1.0 + pre * (1.0 - sigma))
 
+    t_rows[...] = jnp.transpose(recv[0].reshape(768, 512))
+    t_mesh[...] = jnp.transpose(mesh[...])
+    t_act[...] = jnp.transpose(enc_act_sum)
+
     for dy in IN_ORDER:
         arrive(1, dy)
         pre = dot(recv[1, dy], w_ds[...]) + dec_pre[chunk(dy), :]
@@ -395,16 +399,16 @@
         arrive(2, dy)
     mesh_back = dot(t_ds[...], recv[2].reshape(768, 512))
     gmsg = mesh_back.astype(BF16)
-    acc[ENC + 2] = outer(enc_act_sum, gmsg)
+    acc[ENC + 2] = dot(t_act[...], gmsg)
     enc_sums[2].begin()
     high, low = split(dot_back(gmsg, w_eo[...]))
     for dy in range(4):
         back = dot(oh_er[chunk(dy), :], high) + dot(oh_er[chunk(dy), :], low)
         enc_d[chunk(dy), :] = (back * enc_pre[chunk(dy), :]).astype(BF16)
-    acc[ENC + 0] = outer(recv[0].reshape(768, 512), enc_d[...])
+    acc[ENC + 0] = dot(t_rows[...], enc_d[...])
     enc_sums[0].begin()
     mesh_sum = dot(t_er[...], enc_d[...]).astype(BF16)
-    acc[ENC + 1] = outer(mesh[...], mesh_sum)
+    acc[ENC + 1] = dot(t_mesh[...], mesh_sum)
     enc_sums[1].begin()
 
     stores = []
@@ -497,6 +501,9 @@
         pltpu.SemaphoreType.DMA((15,)),
         pltpu.SemaphoreType.DMA((8,)),
         pltpu.VMEM((2, 3, NP, 32), jnp.int32),
+        pltpu.VMEM((512, 768), BF16),
+        pltpu.VMEM((512, 128), BF16),
+        pltpu.VMEM((512, 128), BF16),
         pltpu.VMEM((4, 4, ROWS, 512), BF16),
         pltpu.VMEM((4, 4, ROWS, 512), BF16),
         pltpu.VMEM((768, 256), BF16),

time: 88.5 us -> 88.6 us (level)
  no operation moved by 1% of the time
where the time goes in v5:
time: 88.6 us; the launch traced here: 88.4 us
  Pallas kernels  87.8 us (99%)
    pallas_call x1, Pallas kernels, per_device(): pl.pallas_call(kernel, out_shape=rows + [square] * 6, in_specs=[anywhere]...  82.6 us
    pallas_call x1, Pallas kernels, per_device(): pl.pallas_call(finish, out_shape=rows + [jax.ShapeDtypeStruct((512, 512),...  5.14 us

profile of v5, /device:TPU:1, one launch (start us, length us, event | category | flops | bytes accessed | tf_op | source)
XLA Modules:
  0.0 88.4 jit_solution(13183236055354031645)
XLA Ops:
  0.6 82.6 %shard_map.206 = (f32[256,512]{1,0:T(8,128)}, f32[128,512]{1,0:T(8,128)}, bf16[512,512]{1,0:T(8,128)(2,1)}, bf16[512,512]{1,0:T(8,128)(2,1)}, bf16[512,512]{1,0:...) custom-call(bf16[256,512]{1,0:T(8,128)(2,1)} %grid_in.1, ...), custom_call_target="tpu_custom_call" | custom-call | tf_op jit(solution)/shard_map/pallas_call | solution.py:531
  83.3 5.1 %shard_map.207 = (f32[256,512]{1,0:T(8,128)}, f32[128,512]{1,0:T(8,128)}, f32[512,512]{1,0:T(8,128)}, f32[512,512]{1,0:T(8,128)}, f32[512,512]{1,0:T(8,128)}, /*...) custom-call(f32[256,512]{1,0:T(8,128)} %get-tuple-element.16.grid_in, ...), custom_call_target="tpu_custom_call" | custom-call | tf_op jit(solution)/shard_map/pallas_call | solution.py:546
